TPU v7x, 256 devices: a whole 4x4x8 slice. The times are simulated.
256 devices in a mesh: sta: 32 (over x, z_lo, core), day: 8 (over y, z_hi).
Axes of the slice: x: 4, y: 4, z: 8 (z_hi: 2, z_lo: 4; z = z_hi * 4 + z_lo), core: 2. Of those that a mesh axis runs over, the one named last changes fastest.
Arguments:
- spectra: bfloat16 [32, 2, 32, 3, 1536], P('sta', None, 'day'), may hold values from -1600 to 1600
- flags: int32 [32, 32], P('sta', 'day'), may hold values from 0 to 1
- pair_mask: int32 [32, 32], P('sta'), may hold values 0 or 1
Outputs:
- hourly: bfloat16 [8, 9, 32, 32, 256], P('day', None, 'sta')
- reference_stack: float32 [9, 32, 32, 256], P(None, 'sta', 'day')
All inputs are finite; a program needn't handle non-finite values. No bound on the sum of `pair_mask` on one device may be relied on, other than what follows from the above.
Results may differ from a plain program's by a relative error of at most 0.017.
Values may be sent and summed in bfloat16 or wider, within the bound.
A program may use at most 64 MiB of HBM per device.

v0:
```python
import math

import jax
import jax.numpy as jnp
from jax import lax
from jax.sharding import PartitionSpec as P

LAGS = 256
HALF_BAND = 16


def whiten(spectra, flags):
    values = spectra.astype(jnp.float32)
    bins_count = values.shape[-1]
    power_sum = jnp.sum(values * values, axis=(1, 3))
    padded = jnp.pad(power_sum, ((0, 0), (0, 0), (HALF_BAND, HALF_BAND)))
    smooth = padded[:, :, 0:bins_count]
    for shift_bins in range(1, 2 * HALF_BAND + 1):
        smooth = smooth + padded[:, :, shift_bins : shift_bins + bins_count]
    root_mean = jnp.sqrt(smooth / (6.0 * (2 * HALF_BAND + 1)) + 1e-06)
    good_flags = (1 - flags).astype(jnp.bfloat16)
    scaling = (
        good_flags.astype(jnp.float32)[:, None, :, None, None] / root_mean[:, None, :, None, :]
    )
    return ((values * scaling).astype(jnp.bfloat16), good_flags)


def lag_table(bins_count, lag_count):
    freq_index = jnp.arange(bins_count, dtype=jnp.int32)
    lag_index = jnp.arange(lag_count, dtype=jnp.int32) - lag_count // 2
    phase_step = freq_index[:, None] * lag_index[None, :] % (2 * bins_count)
    phase_angle = phase_step.astype(jnp.float32) * (math.pi / bins_count)
    return jnp.concatenate([jnp.cos(phase_angle), -jnp.sin(phase_angle)], axis=0).astype(
        jnp.bfloat16
    )


def local_side(block, part_index, window):
    return jnp.transpose(block[:, part_index, window], (1, 0, 2))[:, None, :, None, :].astype(
        jnp.float32
    )


def remote_side(block, part_index, window):
    return jnp.transpose(block[:, part_index, window], (1, 0, 2))[None, :, None, :, :].astype(
        jnp.float32
    )


def correlate(local_whit, piece_whit, table_rows):
    bins_count = local_whit.shape[-1]
    windows_here = local_whit.shape[2]
    real_part = None
    imag_part = None
    for window in range(windows_here):
        local_re = local_side(local_whit, 0, window)
        local_im = local_side(local_whit, 1, window)
        piece_re = remote_side(piece_whit, 0, window)
        piece_im = remote_side(piece_whit, 1, window)
        real_term = local_re * piece_re + local_im * piece_im
        imag_term = local_im * piece_re - local_re * piece_im
        real_part = real_term if real_part is None else real_part + real_term
        imag_part = imag_term if imag_part is None else imag_part + imag_term
    real_flat = real_part.astype(jnp.bfloat16).reshape(-1, bins_count)
    imag_flat = imag_part.astype(jnp.bfloat16).reshape(-1, bins_count)
    result = jnp.dot(real_flat, table_rows[:bins_count], preferred_element_type=jnp.float32)
    result = result + jnp.dot(
        imag_flat, table_rows[bins_count:], preferred_element_type=jnp.float32
    )
    result = result * (1.0 / math.sqrt(bins_count))
    return result.reshape(9, local_whit.shape[0], piece_whit.shape[0], table_rows.shape[1])


def on_device(spectra, flags, pair_mask):
    whitened, good_flags = whiten(spectra, flags)
    sta_rows = whitened.shape[0]
    bins_count = whitened.shape[-1]
    station_total = sta_rows * lax.axis_size("sta")
    table_rows = lag_table(bins_count, LAGS)
    piece_whit = lax.all_gather(whitened, "sta", axis=0, tiled=True)
    piece_good = lax.all_gather(good_flags, "sta", axis=0, tiled=True)
    correlation = correlate(whitened, piece_whit, table_rows)
    pair_counts = jnp.dot(good_flags, piece_good.T, preferred_element_type=jnp.float32)
    totals = correlation
    counts = pair_counts
    totals, counts = (totals, counts)
    mask_float = pair_mask.astype(jnp.float32)
    hourly = (
        mask_float[None, :, :, None] * totals / jnp.maximum(counts, 1.0)[None, :, :, None]
    ).astype(jnp.bfloat16)
    share_size = station_total // lax.axis_size("day")
    offset = lax.axis_index("day") * share_size
    day_summed, count_summed = (
        lax.psum(totals.astype(jnp.bfloat16), "day").astype(jnp.float32),
        lax.psum(counts.astype(jnp.bfloat16), "day").astype(jnp.float32),
    )
    day_summed = lax.dynamic_slice_in_dim(day_summed, offset, share_size, 2)
    count_summed = lax.dynamic_slice_in_dim(count_summed, offset, share_size, 1)
    mask_share = lax.dynamic_slice_in_dim(mask_float, offset, share_size, 1)
    reference_stack = (
        mask_share[None, :, :, None] * day_summed / jnp.maximum(count_summed, 1.0)[None, :, :, None]
    )
    return (hourly[None], reference_stack)


def solution(mesh):
    placed = (P("sta", None, "day", None, None), P("sta", "day"), P("sta", None))
    return jax.shard_map(
        on_device,
        mesh=mesh,
        in_specs=placed,
        out_specs=(P("day", None, "sta", None, None), P(None, "sta", "day", None)),
        check_vma=False,
    )
```

profile of v0, /device:TPU:2, one launch (start us, length us, event | category | flops | bytes accessed | tf_op | source)
XLA Modules:
  0.0 216.2 jit_solution(6606771447051726807)
XLA Ops:
  7.2 0.7 convert_bitcast_fusion.10
  7.9 0.9 fusion.10
  8.8 0.5 bitcast_divide_fusion
  9.3 1.6 fusion.11
  10.9 0.0 all-reduce.3.cloned.1.call-start
  10.9 37.2 %all-gather = bf16[32,1,4]{2,1,0:T(2,128)(2,1)S(1)} all-gather(bf16[1,1,4]{2,1,0:T(2,128)(2,1)S(1)} %get-tuple-element.24), channel_id=1, replica_groups=mesh['sta'=32,'day'=8] {'sta'}, dimensions={0}, use_global_device_ids=true | all-gather | bytes 264 | tf_op jit(solution)/shard_map/all_gather | solution.py:81
  48.2 0.1 copy.29
  48.3 0.8 convert_bitcast_fusion.8
  49.0 30.8 %psum.15 = bf16[1,32]{1,0:T(2,128)(2,1)S(1)} all-reduce(bf16[1,32]{1,0:T(2,128)(2,1)S(1)} %get-tuple-element.22), channel_id=1, replica_groups=mesh['sta'=32,'day'=8] {'day'}, use_global_device_ids=true, to_apply=%region_2.3 | all-reduce | flops 32 | bytes 128 | tf_op jit(solution)/shard_map/psum | solution.py:95
  79.8 0.1 fusion.22
  79.9 0.7 fusion.29
  80.6 0.1 fusion.20
  80.7 1.2 slice_convert_fusion.7
  82.0 7.7 %fusion.28 = (bf16[32,1,1,3,1536]{4,2,3,1,0:T(2,128)(2,1)S(1)}, bf16[32,1,1,3,1536]{4,2,3,1,0:T(2,128)(2,1)S(1)}, bf16[32,1,1,3,1536]{4,2,3,1,0:T(2,128)(2,1)S(1...) fusion(bf16[32,2,4,3,1536]{4,2,3,1,0:T(4,128)(2,1)} %all-gather, ...), kind=kLoop, calls=%fused_computation.88 | loop fusion | bytes 4718592 | tf_op jit(solution)/shard_map/slice | solution.py:45
  89.7 0.1 convert_bitcast_fusion.6
  89.8 0.1 convert_bitcast_fusion.4
  89.9 0.1 convert_bitcast_fusion.2
  90.0 0.1 convert_bitcast_fusion
  90.1 1.9 add_convert_fusion
  92.0 6.1 %fusion.9 = f32[288,256]{1,0:T(8,128)S(1)} fusion(bf16[288,1536]{1,0:T(8,128)(2,1)S(1)} %bitcast.112, s32[256]{0:T(256)S(1)} %iota_add_fusion), kind=kOutput, calls=%fused_computation.16 | convolution fusion | flops 230424576 | bytes 1180672 | tf_op jit(solution)/shard_map/dot_general | solution.py:66
  98.1 7.3 %fusion.30 = (bf16[288,256]{1,0:T(8,128)(2,1)}, f32[288,256]{1,0:T(8,128)S(1)}) fusion(f32[288,256]{1,0:T(8,128)S(1)} %fusion.9, bf16[288,1536]{1,0:T(8,128)(2,1)S(1)} %bitcast.111, s32[256]{0:T(256)S(1)} %iota_add_fusion), kind=kOutput, calls=%fused_computation.90 | convolution fusion | flops 231038976 | bytes 1623040 | tf_op jit(solution)/shard_map/dot_general | solution.py:67
  105.4 0.8 divide_convert_fusion
  106.2 101.7 %all-reduce.3.cloned.1.call-done = bf16[9,1,32,256]{3,2,1,0:T(8,128)(2,1)} async-done(((bf16[9,1,32,256]{3,2,1,0:T(8,128)(2,1)}), bf16[9,1,32,256]{3,2,1,0:T(8,128)(2,1)}) %all-reduce.3.cloned.1.call-update) | async-done | bytes 147472 | tf_op jit(solution)/shard_map/psum | solution.py:94
  207.9 1.5 multiply_divide_fusion
  (10 shorter events, 0.2 us)
Async XLA Ops:
  7.2 74.8 %all-gather.3.cloned.1.call-start = ((), (), s32[]{:S(2)}) async-start(), calls=%async_computation | async-start | bytes 2433024 | tf_op jit(solution)/shard_map/all_gather | solution.py:80
  10.9 197.0 %all-reduce.3.cloned.1.call-start = ((), (), s32[]{:S(2)}) async-start(), calls=%async_computation.1 | async-start | bytes 294912 | tf_op jit(solution)/shard_map/psum | solution.py:94
Sparse Core Ops, SparseCore 0:
  11.0 63.5 all-gather.2
  105.5 102.3 all-reduce.2
where the time goes:
time: 217 us; the launch traced here: 216 us
  waiting for transfers between devices  102 us (47%)
  blocking collectives  68 us (31%)
  matrix products  14.2 us (7%)
  between operations  14.2 us (7%)
  other arithmetic  10 us (5%)
  local copies, waits for them, and re-layouts  7.94 us (4%)
    psum x1, waiting for transfers between devices, on_device(): lax.psum(totals.astype(jnp.bfloat16), 'day').astype(jnp.float32)  102 us
    all_gather x1, blocking collectives, on_device(): piece_good = lax.all_gather(good_flags, 'sta', axis=0, tiled=True)  37.2 us
    psum x1, blocking collectives, on_device(): lax.psum(counts.astype(jnp.bfloat16), 'day').astype(jnp.float32)  30.8 us
    slice x1, local copies, waits for them, and re-layouts, remote_side(): block[:, part_index, window]  7.72 us
    dot_general x1, matrix products, correlate(): jnp.dot(imag_flat, table_rows[bins_count:], preferred_element_type=jnp.fl...  7.28 us
    dot_general x1, matrix products, correlate(): jnp.dot(real_flat, table_rows[:bins_count], preferred_element_type=jnp.fl...  6.1 us
  transfers between devices with their start and end apart: 2, of which 1 were waited for; matrix products, arithmetic and copies ran while one was open for 2% of the time, Pallas kernels for 0%

commit v1 on v0

v1 whole, which is shorter than its diff:
```python
import math

import jax
import jax.numpy as jnp
import ml_dtypes
import numpy as np
from jax import lax
from jax.experimental import pallas as pl
from jax.experimental.pallas import tpu as pltpu
from jax.sharding import PartitionSpec as P

BINS = 1536
LAGS = 256
HALF_BAND = 16
WIN = 4
LANES = 128
FC = BINS // LANES
ROWS_FC = 24
FLAG_ROWS = 16
ROWS = FLAG_ROWS + FC * ROWS_FC
NC = 3
FCC = FC // NC
BOUNDS = [0] + [FLAG_ROWS + (k + 1) * FCC * ROWS_FC for k in range(NC)]
PAD = 128
MESH = pl.DeviceIdType.MESH


def lag_table():
    freq = np.arange(BINS, dtype=np.int64)
    lag = np.arange(LAGS, dtype=np.int64) - LAGS // 2
    angle = (freq[:, None] * lag[None, :] % (2 * BINS)) * (math.pi / BINS)
    parts = np.stack([np.cos(angle), -np.sin(angle)]).reshape(2, FC, LANES, LAGS)
    rows = np.transpose(parts, (1, 0, 2, 3)).reshape(2 * BINS, LAGS)
    return rows.astype(np.float32).astype(ml_dtypes.bfloat16)


def kernel(
    spec_ref, flags_ref, mask_ref, table_hbm,
    hourly_ref, stack_ref,
    power, white, t_blocks, s_blocks, t_wide, s_wide, table, products, total,
    mask_col, wide, hour_send, hour_recv, ref_send, ref_recv, hour_wide,
    table_sem, zs, zr, xs, xr, cs, cr, hs, hr, rs, rr,
):
    sta = lax.axis_index("sta")
    day = lax.axis_index("day")
    x0, z0, c0 = sta // 8, (sta // 2) % 4, sta % 2
    y0, h0 = day // 2, day % 2

    def sta_of(x, z, c):
        return (x * 4 + z) * 2 + c

    def at(x, z, c, d):
        return (sta_of(x, z, c), d)

    sibling = at(x0, z0, 1 - c0, day)

    barrier = pltpu.get_barrier_semaphore()

    def greet(target):
        pl.semaphore_signal(barrier, inc=1, device_id=target, device_id_type=MESH)

    for step in (1, 2, 3):
        greet(at((x0 + step) % 4, z0, c0, day))
        greet(at(x0, (z0 + step) % 4, c0, day))
    greet(sibling)
    mine = x0 == y0
    for d in range(8):

        @pl.when(jnp.logical_not(jnp.logical_and(mine, d == day)))
        def _():
            greet(at(y0, z0, c0, d))

    table_copy = pltpu.make_async_copy(table_hbm, table, table_sem)
    table_copy.start()

    power[...] = jnp.zeros_like(power)
    for w in range(WIN):
        re = spec_ref[0, 0, w].astype(jnp.float32)
        im = spec_ref[0, 1, w].astype(jnp.float32)
        q = re * re + im * im
        power[w : w + 1, 0:BINS] = q[0:1] + q[1:2] + q[2:3]
    single = power[...]
    span = single
    for shift in (1, 2, 4, 8, 16):
        span = span + pltpu.roll(span, shift, axis=1)
    span = span + pltpu.roll(single, 2 * HALF_BAND, axis=1)
    smooth = pltpu.roll(span, BINS + PAD - HALF_BAND, axis=1)[:, 0:BINS]
    scale = lax.rsqrt(smooth / (6.0 * (2 * HALF_BAND + 1)) + 1e-06)
    for w in range(WIN):
        good = (1 - flags_ref[0, w]).astype(jnp.float32)
        row = scale[w : w + 1] * good
        for part in range(2):
            y = spec_ref[0, part, w].astype(jnp.float32) * row
            first = FLAG_ROWS + (part * WIN + w) * 3
            for fc in range(FC):
                white[first + fc * ROWS_FC : first + fc * ROWS_FC + 3, :] = y[
                    :, fc * LANES : (fc + 1) * LANES
                ]
        white[w : w + 1, :] = jnp.full((1, LANES), good)
    white[WIN:FLAG_ROWS, :] = jnp.zeros((FLAG_ROWS - WIN, LANES), jnp.float32)
    block = white[...].astype(jnp.bfloat16)
    own = z0 * 2 + c0
    t_blocks[own] = block
    s_blocks[x0] = block

    line = lax.broadcasted_iota(jnp.int32, (32, 32), 0)
    place = lax.broadcasted_iota(jnp.int32, (32, 32), 1)
    spread = jnp.broadcast_to(mask_ref[...].astype(jnp.float32), (32, 32))
    column = jnp.sum(jnp.where(line == place, spread, 0.0), axis=1, keepdims=True)
    mask_col[...] = jnp.broadcast_to(column, (32, LAGS))

    pl.semaphore_wait(barrier, 15 - mine.astype(jnp.int32))

    def piece(ref, slot, k):
        return ref.at[slot, pl.ds(BOUNDS[k], BOUNDS[k + 1] - BOUNDS[k]), :]

    def z_copy(step, k, slot):
        return pltpu.make_async_remote_copy(
            src_ref=piece(t_blocks, own, k),
            dst_ref=piece(t_blocks, slot, k),
            send_sem=zs.at[step, k],
            recv_sem=zr.at[step, k],
            device_id=at(x0, (z0 + step) % 4, c0, day),
            device_id_type=MESH,
        )

    def x_copy(step, k, slot):
        return pltpu.make_async_remote_copy(
            src_ref=piece(s_blocks, x0, k),
            dst_ref=piece(s_blocks, slot, k),
            send_sem=xs.at[step, k],
            recv_sem=xr.at[step, k],
            device_id=at((x0 + step) % 4, z0, c0, day),
            device_id_type=MESH,
        )

    def core_copy(step, k, core):
        slot = ((z0 - step + 4) % 4) * 2 + core
        return pltpu.make_async_remote_copy(
            src_ref=piece(t_blocks, slot, k),
            dst_ref=piece(t_blocks, slot, k),
            send_sem=cs.at[step, k],
            recv_sem=cr.at[step, k],
            device_id=sibling,
            device_id_type=MESH,
        )

    for k in range(NC):
        for step in (2, 1, 3):
            z_copy(step, k, own).start()
        for step in (2, 1, 3):
            x_copy(step, k, x0).start()
        core_copy(0, k, c0).start()

    table_copy.wait()
    for k in range(NC):
        for step in (1, 3, 2):
            z_copy(step, k, ((z0 - step + 4) % 4) * 2 + c0).wait_recv()
            core_copy(step, k, c0).start()
        for step in (1, 3, 2):
            x_copy(step, k, (x0 - step + 4) % 4).wait_recv()
        for step in range(4):
            core_copy(step, k, 1 - c0).wait_recv()
        low, high = BOUNDS[k], BOUNDS[k + 1]
        for slot in range(8):
            t_wide[slot * ROWS + low : slot * ROWS + high, :] = t_blocks[slot, low:high].astype(
                jnp.float32
            )
        for slot in range(4):
            s_wide[slot * ROWS + low : slot * ROWS + high, :] = s_blocks[slot, low:high].astype(
                jnp.float32
            )

        def cross(i, carry):
            fc = k * FCC + i
            base = FLAG_ROWS + fc * ROWS_FC
            t = [t_wide[pl.ds(base + r, 8, stride=ROWS), :] for r in range(ROWS_FC)]
            column = pl.multiple_of(fc * 2 * LANES, 2 * LANES)
            for pair in range(6):
                re_tiles, im_tiles = [], []
                for sa in (2 * pair, 2 * pair + 1):
                    s, a = divmod(sa, 3)
                    local = [
                        jnp.broadcast_to(
                            s_wide[pl.ds(s * ROWS + base + r * 3 + a, 1), :], (8, LANES)
                        )
                        for r in range(2 * WIN)
                    ]
                    for b in range(3):
                        re, im = None, None
                        for w in range(WIN):
                            t_re, t_im = t[w * 3 + b], t[(WIN + w) * 3 + b]
                            re_term = local[w] * t_re + local[WIN + w] * t_im
                            im_term = local[WIN + w] * t_re - local[w] * t_im
                            re = re_term if re is None else re + re_term
                            im = im_term if im is None else im + im_term
                        re_tiles.append(re)
                        im_tiles.append(im)
                rows = pl.ds(pair * 48, 48)
                products[rows, pl.ds(column, LANES)] = jnp.concatenate(re_tiles, axis=0).astype(
                    jnp.bfloat16
                )
                products[rows, pl.ds(column + LANES, LANES)] = jnp.concatenate(
                    im_tiles, axis=0
                ).astype(jnp.bfloat16)
            return carry

        lax.fori_loop(0, FCC, cross, 0)
        depth = FCC * 2 * LANES
        term = jnp.dot(
            products[:, k * depth : (k + 1) * depth],
            table[k * depth : (k + 1) * depth, :],
            preferred_element_type=jnp.float32,
        )
        total[...] = term if k == 0 else total[...] + term

    def hour_copy(step, slot):
        return pltpu.make_async_remote_copy(
            src_ref=hour_send.at[step],
            dst_ref=hour_recv.at[slot],
            send_sem=hs.at[step],
            recv_sem=hr.at[step],
            device_id=at((x0 + step) % 4, z0, c0, day),
            device_id_type=MESH,
        )

    def ref_copy(step, other, slot):
        return pltpu.make_async_remote_copy(
            src_ref=ref_send.at[step, other],
            dst_ref=ref_recv.at[slot],
            send_sem=rs.at[step, other],
            recv_sem=rr.at[slot],
            device_id=at((x0 + step) % 4, z0, c0, x0 * 2 + (h0 + other) % 2),
            device_id_type=MESH,
        )

    for step in (2, 1, 3, 0):
        s = (x0 + step) % 4
        first = pl.multiple_of(s * 72, 8)
        first_s = pl.multiple_of(s * ROWS, 8)
        count = None
        for w in range(WIN):
            g = s_wide[pl.ds(first_s + w, 1), :] * t_wide[pl.ds(w, 8, stride=ROWS), :]
            count = g if count is None else count + g
        whole = jnp.concatenate(
            [
                total[pl.ds(first, 72), :] * (1.0 / math.sqrt(BINS)),
                jnp.concatenate([count, count], axis=1),
            ],
            axis=0,
        )
        for side in range(2):
            for half in range(2):
                for p in range(10):
                    wide[side, half * 40 + p * 4 : half * 40 + p * 4 + 4, :] = whole[
                        p * 8 + side * 4 : p * 8 + side * 4 + 4, half * LANES : (half + 1) * LANES
                    ]
        for other in range(2):
            ref_send[step, other] = wide[(h0 + other) % 2].astype(jnp.bfloat16)
        if step == 0:
            hour_recv[x0] = whole.astype(jnp.bfloat16)

            @pl.when(mine)
            def _():
                ref_recv[day] = ref_send[0, 0]

            @pl.when(jnp.logical_not(mine))
            def _():
                ref_copy(0, 0, day).start()

            ref_copy(0, 1, day).start()
        else:
            hour_send[step] = whole.astype(jnp.bfloat16)
            for other in (1, 0):
                ref_copy(step, other, day).start()
            hour_copy(step, x0).start()

    for step in (0, 1, 3, 2):
        x = (x0 - step + 4) % 4
        if step:
            hour_copy(step, x).wait_recv()
        got = hour_recv[x].astype(jnp.float32)
        rows = pl.ds(pl.multiple_of(x * 8, 8), 8)
        factor = mask_col[rows, :] / jnp.maximum(got[72:80], 1.0)
        for p in range(9):
            hour_wide[p, rows, :] = got[p * 8 : p * 8 + 8] * factor
    for p in range(9):
        hourly_ref[0, p, 0] = hour_wide[p].astype(jnp.bfloat16)

    for d in range(8):

        @pl.when(jnp.logical_not(jnp.logical_and(mine, d == day)))
        def _():
            ref_copy(1, 0, d).wait_recv()

    summed = ref_recv[0].astype(jnp.float32)
    for d in range(1, 8):
        summed = summed + ref_recv[d].astype(jnp.float32)
    mask8 = mask_col[pl.ds(pl.multiple_of(y0 * 8, 8), 8), 0:LANES]
    mask4 = jnp.where(h0 == 0, mask8[0:4], mask8[4:8])
    for half in range(2):
        part = summed[half * 40 : half * 40 + 40]
        factor = mask4 / jnp.maximum(part[36:40], 1.0)
        for p in range(9):
            stack_ref[p, 0, :, half * LANES : (half + 1) * LANES] = part[p * 4 : p * 4 + 4] * factor

    for k in range(NC):
        for step in (1, 2, 3):
            z_copy(step, k, own).wait_send()
            x_copy(step, k, x0).wait_send()
        for step in range(4):
            core_copy(step, k, c0).wait_send()
    for step in range(4):
        if step:
            hour_copy(step, x0).wait_send()
            ref_copy(step, 0, day).wait_send()
        else:

            @pl.when(jnp.logical_not(mine))
            def _():
                ref_copy(0, 0, day).wait_send()

        ref_copy(step, 1, day).wait_send()


def on_device(spectra, flags, pair_mask):
    table = jnp.asarray(lag_table())
    bf16, f32 = jnp.bfloat16, jnp.float32
    dma = pltpu.SemaphoreType.DMA
    vmem = pltpu.VMEM
    return pl.pallas_call(
        kernel,
        out_shape=(
            jax.ShapeDtypeStruct((1, 9, 1, 32, LAGS), bf16),
            jax.ShapeDtypeStruct((9, 1, 4, LAGS), f32),
        ),
        in_specs=[
            pl.BlockSpec(memory_space=pltpu.VMEM),
            pl.BlockSpec(memory_space=pltpu.SMEM),
            pl.BlockSpec(memory_space=pltpu.VMEM),
            pl.BlockSpec(memory_space=pl.ANY),
        ],
        out_specs=(
            pl.BlockSpec(memory_space=pltpu.VMEM),
            pl.BlockSpec(memory_space=pltpu.VMEM),
        ),
        scratch_shapes=[
            vmem((8, BINS + PAD), f32),
            vmem((ROWS, LANES), f32),
            vmem((8, ROWS, LANES), bf16),
            vmem((4, ROWS, LANES), bf16),
            vmem((8 * ROWS, LANES), f32),
            vmem((4 * ROWS, LANES), f32),
            vmem((2 * BINS, LAGS), bf16),
            vmem((288, 2 * BINS), bf16),
            vmem((288, LAGS), f32),
            vmem((32, LAGS), f32),
            vmem((2, 80, LANES), f32),
            vmem((4, 80, LAGS), bf16),
            vmem((4, 80, LAGS), bf16),
            vmem((4, 2, 80, LANES), bf16),
            vmem((8, 80, LANES), bf16),
            vmem((9, 32, LAGS), f32),
            dma,
            dma((4, NC)),
            dma((4, NC)),
            dma((4, NC)),
            dma((4, NC)),
            dma((4, NC)),
            dma((4, NC)),
            dma((4,)),
            dma((4,)),
            dma((4, 2)),
            dma((8,)),
        ],
        compiler_params=pltpu.CompilerParams(
            collective_id=0, has_side_effects=True, vmem_limit_bytes=32 * 1024 * 1024
        ),
        cost_estimate=pl.CostEstimate(
            flops=500_000_000, bytes_accessed=2_000_000, transcendentals=6144
        ),
    )(spectra, flags, pair_mask, table)


def solution(mesh):
    placed = (P("sta", None, "day", None, None), P("sta", "day"), P("sta", None))
    return jax.shard_map(
        on_device,
        mesh=mesh,
        in_specs=placed,
        out_specs=(P("day", None, "sta", None, None), P(None, "sta", "day", None)),
        check_vma=False,
    )
```

time: 217 us -> 37.5 us (0.17)
  the two profiles are of different devices: /device:TPU:2 before, /device:TPU:1 now
where the time goes in v1:
time: 37.5 us; the launch traced here: 37.3 us
  Pallas kernels  31.7 us (85%)
  local copies, waits for them, and re-layouts  4.92 us (13%)
  between operations  0.65 us (2%)
    pallas_call x1, Pallas kernels, on_device(): pl.pallas_call(kernel, out_shape=(jax.ShapeDtypeStruct((1, 9, 1, 32, LAGS...  31.7 us
    unnamed x9, local copies, waits for them, and re-layouts  4.92 us

profile of v1, /device:TPU:1, one launch (start us, length us, event | category | flops | bytes accessed | tf_op | source)
XLA Modules:
  0.0 37.3 jit_solution(503115872847447591)
XLA Ops:
  0.6 0.9 %copy.6.spec_ref = bf16[1,2,4,3,1536]{4,3,2,1,0:T(4,128)(2,1)S(1)} copy(bf16[1,2,4,3,1536]{4,2,3,1,0:T(4,128)(2,1)} %param.4) | data formatting | bytes 147456 | tf_op args[0]
  1.6 0.0 copy-start
  1.6 0.6 %copy-done = s32[1,4]{1,0:T(1,128)S(1)} copy-done((s32[1,4]{1,0:T(1,128)S(1)}, s32[1,4]{1,0:T(1,128)}, u32[]{:S(2)}) %copy-start) | copy-done | bytes 40
  2.2 0.0 copy-start.1
  2.2 0.7 %copy-done.1 = s32[1,32]{1,0:T(1,128)S(1)} copy-done((s32[1,32]{1,0:T(1,128)S(1)}, s32[1,32]{1,0:T(1,128)}, u32[]{:S(2)}) %copy-start.1) | copy-done | bytes 152
  2.9 0.0 copy-start.2
  2.9 1.4 %copy-done.2 = bf16[3072,256]{1,0:T(8,128)(2,1)S(1)} copy-done((bf16[3072,256]{1,0:T(8,128)(2,1)S(1)}, bf16[3072,256]{1,0:T(8,128)(2,1)}, u32[]{:S(2)}) %copy-start.2) | copy-done | bytes 1572888
  4.3 31.7 %shard_map.59 = (bf16[1,9,1,32,256]{4,3,2,1,0:T(8,128)(2,1)S(1)}, f32[9,1,4,256]{3,2,1,0:T(4,128)S(1)}) custom-call(bf16[1,2,4,3,1536]{4,3,2,1,0:T(4,128)(2,1)S(1)} %copy.6.spec_ref, s32[1,4]{1,0:T(1,128)S(1)} %copy-done, s32[1,32]{1,0:T(1,128)S(1)} %copy-done.1, bf16[3072,256]{1,0:T(8,128)(2,1)S(1)} %copy-done.2), custom_call_target="tpu_custom_call" | custom-call | flops 500000000 | bytes 2000000 | tf_op jit(solution)/shard_map/pallas_call | solution.py:331
  36.0 0.7 %copy.9 = bf16[1,9,1,32,256]{4,3,2,1,0:T(8,128)(2,1)} copy(bf16[1,9,1,32,256]{4,3,2,1,0:T(8,128)(2,1)S(1)} %get-tuple-element.4) | data formatting | bytes 294912
  36.7 0.6 %copy.10 = f32[9,1,4,256]{3,2,1,0:T(4,128)} copy(f32[9,1,4,256]{3,2,1,0:T(4,128)S(1)} %get-tuple-element.5) | data formatting | bytes 73728
Async XLA Ops:
  1.6 0.7 %copy-start = (s32[1,4]{1,0:T(1,128)S(1)}, s32[1,4]{1,0:T(1,128)}, u32[]{:S(2)}) copy-start(s32[1,4]{1,0:T(1,128)} %flags_ref.1) | copy-start | bytes 52
  2.2 0.7 %copy-start.1 = (s32[1,32]{1,0:T(1,128)S(1)}, s32[1,32]{1,0:T(1,128)}, u32[]{:S(2)}) copy-start(s32[1,32]{1,0:T(1,128)} %mask_ref.1) | copy-start | bytes 388
  2.9 1.4 %copy-start.2 = (bf16[3072,256]{1,0:T(8,128)(2,1)S(1)}, bf16[3072,256]{1,0:T(8,128)(2,1)}, u32[]{:S(2)}) copy-start(bf16[3072,256]{1,0:T(8,128)(2,1)} %constant.2.clone.table_hbm) | copy-start | bytes 4718596

commit v2 on v1

v2 whole, which is shorter than its diff:
```python
import math

import jax
import jax.numpy as jnp
import ml_dtypes
import numpy as np
from jax import lax
from jax.experimental import pallas as pl
from jax.experimental.pallas import tpu as pltpu
from jax.sharding import PartitionSpec as P

BINS = 1536
LAGS = 256
HALF_BAND = 16
WIN = 4
LANES = 128
FC = BINS // LANES
ROWS_FC = 24
FLAG_ROWS = 16
ROWS = FLAG_ROWS + FC * ROWS_FC
NC = 3
FCC = FC // NC
BOUNDS = [0] + [FLAG_ROWS + (k + 1) * FCC * ROWS_FC for k in range(NC)]
PAD = 128
MESH = pl.DeviceIdType.MESH


def lag_table():
    freq = np.arange(BINS, dtype=np.int64)
    lag = np.arange(LAGS, dtype=np.int64) - LAGS // 2
    angle = (freq[:, None] * lag[None, :] % (2 * BINS)) * (math.pi / BINS)
    parts = np.stack([np.cos(angle), -np.sin(angle)]).reshape(2, FC, LANES, LAGS)
    rows = np.transpose(parts, (1, 0, 2, 3)).reshape(2 * BINS, LAGS)
    return rows.astype(np.float32).astype(ml_dtypes.bfloat16)


def kernel(
    spec_hbm, flags_hbm, mask_hbm, table_hbm,
    hourly_ref, stack_ref,
    spec_ref, flags_ref, mask_ref, power, white, t_blocks, s_blocks, t_wide, s_wide, table, products, total,
    mask_col, mask_own, wide, hour_send, hour_recv, ref_send, ref_recv, ref_wide,
    in_sems, table_sem, zs, zr, fs, xs, xr, cs, cr, hs, hr, rs, rr, ready,
):
    sta = lax.axis_index("sta")
    day = lax.axis_index("day")
    x0, z0, c0 = sta // 8, (sta // 2) % 4, sta % 2
    y0, h0 = day // 2, day % 2

    def sta_of(x, z, c):
        return (x * 4 + z) * 2 + c

    def at(x, z, c, d):
        return (sta_of(x, z, c), d)

    sibling = at(x0, z0, 1 - c0, day)

    loads = [
        pltpu.make_async_copy(spec_hbm, spec_ref, in_sems.at[0]),
        pltpu.make_async_copy(flags_hbm, flags_ref, in_sems.at[1]),
        pltpu.make_async_copy(mask_hbm, mask_ref, in_sems.at[2]),
    ]
    for load in loads:
        load.start()
    table_copy = pltpu.make_async_copy(table_hbm, table, table_sem)
    table_copy.start()

    barrier = pltpu.get_barrier_semaphore()

    def greet(target):
        pl.semaphore_signal(barrier, inc=1, device_id=target, device_id_type=MESH)

    for step in (1, 2, 3):
        greet(at((x0 + step) % 4, z0, c0, day))
        greet(at(x0, (z0 + step) % 4, c0, day))
    greet(sibling)
    mine = x0 == y0
    early = h0 == 0
    for y in range(4):

        @pl.when(jnp.logical_not(jnp.logical_and(mine, y == y0)))
        def _():
            greet(at(y0, z0, c0, y * 2 + h0))

        @pl.when(early)
        def _():
            greet(at(y0, z0, c0, y * 2 + 1))
            greet(at(y, z0, c0, x0 * 2 + 1))

    loads[0].wait()
    loads[1].wait()
    power[...] = jnp.zeros_like(power)
    energy = None
    for part in range(2):
        for comp in range(3):
            values = spec_ref[0, part, comp].astype(jnp.float32)
            energy = values * values if energy is None else energy + values * values
    power[0:WIN, 0:BINS] = energy
    single = power[...]
    span = single
    for shift in (1, 2, 4, 8, 16):
        span = span + pltpu.roll(span, shift, axis=1)
    span = span + pltpu.roll(single, 2 * HALF_BAND, axis=1)
    smooth = pltpu.roll(span, BINS + PAD - HALF_BAND, axis=1)[0:WIN, 0:BINS]
    line = lax.broadcasted_iota(jnp.int32, (WIN, WIN), 0)
    place = lax.broadcasted_iota(jnp.int32, (WIN, WIN), 1)
    spread = jnp.broadcast_to((1 - flags_ref[...]).astype(jnp.float32), (WIN, WIN))
    good = jnp.sum(jnp.where(line == place, spread, 0.0), axis=1, keepdims=True)
    scale = lax.rsqrt(smooth / (6.0 * (2 * HALF_BAND + 1)) + 1e-06) * good
    for part in range(2):
        for comp in range(3):
            y = spec_ref[0, part, comp].astype(jnp.float32) * scale
            first = FLAG_ROWS + (part * 3 + comp) * WIN
            for fc in range(FC):
                white[first + fc * ROWS_FC : first + fc * ROWS_FC + WIN, :] = y[
                    :, fc * LANES : (fc + 1) * LANES
                ]
    white[0:WIN, :] = jnp.broadcast_to(good, (WIN, LANES))
    white[WIN:FLAG_ROWS, :] = jnp.zeros((FLAG_ROWS - WIN, LANES), jnp.float32)
    block = white[...].astype(jnp.bfloat16)
    own = z0 * 2 + c0
    t_blocks[own] = block
    s_blocks[x0] = block

    loads[2].wait()
    spread = jnp.broadcast_to(mask_ref[...].astype(jnp.float32), (32, 32))
    line = lax.broadcasted_iota(jnp.int32, (32, 32), 0)
    place = lax.broadcasted_iota(jnp.int32, (32, 32), 1)
    column = jnp.sum(jnp.where(line == place, spread, 0.0), axis=1, keepdims=True)
    mask_col[...] = jnp.broadcast_to(column, (32, LANES))
    column = jnp.sum(
        jnp.where(line[0:8] + day * 4 == place[0:8], spread[0:8], 0.0), axis=1, keepdims=True
    )
    mask_own[...] = jnp.broadcast_to(column, (8, LANES))

    @pl.when(early)
    def _():
        pl.semaphore_wait(barrier, 11 - mine.astype(jnp.int32))

    @pl.when(jnp.logical_not(early))
    def _():
        pl.semaphore_wait(barrier, 19 - mine.astype(jnp.int32))
        for y in range(4):
            pl.semaphore_signal(
                ready, inc=1, device_id=at(y0, z0, c0, y * 2), device_id_type=MESH
            )


    def piece(ref, slot, k):
        return ref.at[slot, pl.ds(BOUNDS[k], BOUNDS[k + 1] - BOUNDS[k]), :]

    def z_copy(step, k, slot):
        return pltpu.make_async_remote_copy(
            src_ref=piece(t_blocks, own, k),
            dst_ref=piece(t_blocks, slot, k),
            send_sem=zs.at[step, k],
            recv_sem=zr.at[step, k],
            device_id=at(x0, (z0 + step) % 4, c0, day),
            device_id_type=MESH,
        )

    def relay(k, slot, z):
        return pltpu.make_async_remote_copy(
            src_ref=piece(t_blocks, slot, k),
            dst_ref=piece(t_blocks, slot, k),
            send_sem=fs.at[k],
            recv_sem=zr.at[2, k],
            device_id=at(x0, z, c0, day),
            device_id_type=MESH,
        )

    def x_copy(step, k, slot):
        return pltpu.make_async_remote_copy(
            src_ref=piece(s_blocks, x0, k),
            dst_ref=piece(s_blocks, slot, k),
            send_sem=xs.at[step, k],
            recv_sem=xr.at[step, k],
            device_id=at((x0 + step) % 4, z0, c0, day),
            device_id_type=MESH,
        )

    def core_copy(step, k, core):
        slot = ((z0 - step + 4) % 4) * 2 + core
        return pltpu.make_async_remote_copy(
            src_ref=piece(t_blocks, slot, k),
            dst_ref=piece(t_blocks, slot, k),
            send_sem=cs.at[step, k],
            recv_sem=cr.at[step, k],
            device_id=sibling,
            device_id_type=MESH,
        )

    outer = jnp.logical_or(z0 == 0, z0 == 3)
    inner = jnp.logical_not(outer)

    for k in range(NC):
        for step in (1, 3):
            z_copy(step, k, own).start()

        @pl.when(outer)
        def _():
            z_copy(2, k, own).start()

        for step in (2, 1, 3):
            x_copy(step, k, x0).start()
        core_copy(0, k, c0).start()

    table_copy.wait()
    for k in range(NC):

        @pl.when(z0 == 2)
        def _():
            z_copy(1, k, 2 + c0).wait_recv()
            relay(k, 2 + c0, 3).start()
            core_copy(1, k, c0).start()

        @pl.when(z0 == 1)
        def _():
            z_copy(3, k, 4 + c0).wait_recv()
            relay(k, 4 + c0, 0).start()
            core_copy(3, k, c0).start()

    for k in range(NC):
        @pl.when(z0 != 2)
        def _():
            z_copy(1, k, ((z0 + 3) % 4) * 2 + c0).wait_recv()
            core_copy(1, k, c0).start()

        @pl.when(z0 != 1)
        def _():
            z_copy(3, k, ((z0 + 1) % 4) * 2 + c0).wait_recv()
            core_copy(3, k, c0).start()

        z_copy(2, k, ((z0 + 2) % 4) * 2 + c0).wait_recv()
        core_copy(2, k, c0).start()
        for step in (1, 3, 2):
            x_copy(step, k, (x0 - step + 4) % 4).wait_recv()
        for step in range(4):
            core_copy(step, k, 1 - c0).wait_recv()
        low, high = BOUNDS[k], BOUNDS[k + 1]
        for slot in range(8):
            t_wide[slot * ROWS + low : slot * ROWS + high, :] = t_blocks[slot, low:high].astype(
                jnp.float32
            )
        for slot in range(4):
            s_wide[slot * ROWS + low : slot * ROWS + high, :] = s_blocks[slot, low:high].astype(
                jnp.float32
            )

        def cross(i, carry):
            fc = k * FCC + i
            base = FLAG_ROWS + fc * ROWS_FC
            t = [t_wide[pl.ds(base + r, 8, stride=ROWS), :] for r in range(ROWS_FC)]
            column = pl.multiple_of(fc * 2 * LANES, 2 * LANES)
            for pair in range(6):
                re_tiles, im_tiles = [], []
                for sa in (2 * pair, 2 * pair + 1):
                    s, a = divmod(sa, 3)
                    local = [
                        jnp.broadcast_to(
                            s_wide[pl.ds(s * ROWS + base + (part * 3 + a) * WIN + w, 1), :],
                            (8, LANES),
                        )
                        for part in range(2)
                        for w in range(WIN)
                    ]
                    for b in range(3):
                        re, im = None, None
                        for w in range(WIN):
                            t_re, t_im = t[b * WIN + w], t[(3 + b) * WIN + w]
                            re_term = local[w] * t_re + local[WIN + w] * t_im
                            im_term = local[WIN + w] * t_re - local[w] * t_im
                            re = re_term if re is None else re + re_term
                            im = im_term if im is None else im + im_term
                        re_tiles.append(re)
                        im_tiles.append(im)
                rows = pl.ds(pair * 48, 48)
                products[rows, pl.ds(column, LANES)] = jnp.concatenate(re_tiles, axis=0).astype(
                    jnp.bfloat16
                )
                products[rows, pl.ds(column + LANES, LANES)] = jnp.concatenate(
                    im_tiles, axis=0
                ).astype(jnp.bfloat16)
            return carry

        lax.fori_loop(0, FCC, cross, 0)
        depth = FCC * 2 * LANES
        term = jnp.dot(
            products[:, k * depth : (k + 1) * depth],
            table[k * depth : (k + 1) * depth, :],
            preferred_element_type=jnp.float32,
        )
        total[...] = term if k == 0 else total[...] + term

    def hour_copy(step, slot):
        return pltpu.make_async_remote_copy(
            src_ref=hour_send.at[step],
            dst_ref=hour_recv.at[slot],
            send_sem=hs.at[step],
            recv_sem=hr.at[step],
            device_id=at((x0 + step) % 4, z0, c0, day),
            device_id_type=MESH,
        )

    def ref_copy(step, h, slot):
        return pltpu.make_async_remote_copy(
            src_ref=ref_send.at[step, h],
            dst_ref=ref_recv.at[slot],
            send_sem=rs.at[step, h],
            recv_sem=rr.at[slot],
            device_id=at((x0 + step) % 4, z0, c0, x0 * 2 + h),
            device_id_type=MESH,
        )

    for step in (2, 1, 3, 0):
        x = (x0 + step) % 4
        first_s = pl.multiple_of(x * ROWS, 8)
        count = None
        for w in range(WIN):
            g = s_wide[pl.ds(first_s + w, 1), :] * t_wide[pl.ds(w, 8, stride=ROWS), :]
            count = g if count is None else count + g
        scaled = total[pl.ds(pl.multiple_of(x * 72, 8), 72), :] * (1.0 / math.sqrt(BINS))
        for half in range(2):
            first = step * 160 + half * 80
            wide[first : first + 72, :] = scaled[:, half * LANES : (half + 1) * LANES]
            wide[first + 72 : first + 80, :] = count
        for h in range(2):
            first = step * 160 + h * 4
            tiles = [
                wide[pl.ds(first + q * 64 + j, 8, stride=8), :] for j in range(4) for q in range(2)
            ] + [wide[pl.ds(first + 128 + j, 4, stride=8), :] for j in range(4)]
            ref_send[step, h] = jnp.concatenate(tiles, axis=0).astype(jnp.bfloat16)

        @pl.when(jnp.logical_not(early))
        def _():
            ref_copy(step, 0, day).start()

    def send_ref(step, h):
        if step:
            ref_copy(step, h, day).start()
        else:
            local = jnp.logical_and(mine, h0 == h)

            @pl.when(local)
            def _():
                ref_recv[day] = ref_send[0, h]

            @pl.when(jnp.logical_not(local))
            def _():
                ref_copy(0, h, day).start()

    @pl.when(early)
    def _():
        for step in (2, 1, 3, 0):
            send_ref(step, 0)

    @pl.when(jnp.logical_not(early))
    def _():
        for step in (2, 1, 3, 0):
            send_ref(step, 1)

    for step in (2, 1, 3, 0):
        message = wide[step * 160 : step * 160 + 160, :].astype(jnp.bfloat16)
        if step:
            hour_send[step] = message
            hour_copy(step, x0).start()
        else:
            hour_recv[x0] = message

    @pl.when(early)
    def _():
        pl.semaphore_wait(ready, 4)
        for step in (2, 1, 3, 0):
            ref_copy(step, 1, day).start()

    for step in (0, 1, 3, 2):
        x = (x0 - step + 4) % 4
        if step:
            hour_copy(step, x).wait_recv()
    for pair in range(2):
        for half in range(2):
            first = half * 80
            got = [
                hour_recv[pair * 2 + i, first : first + 80, :].astype(jnp.float32) for i in range(2)
            ]
            factors = [
                mask_col[pair * 16 + i * 8 : pair * 16 + i * 8 + 8, :]
                / jnp.maximum(got[i][72:80], 1.0)
                for i in range(2)
            ]
            for p in range(9):
                tiles = [got[i][p * 8 : p * 8 + 8] * factors[i] for i in range(2)]
                hourly_ref[
                    0, p, 0, pair * 16 : pair * 16 + 16, half * LANES : (half + 1) * LANES
                ] = jnp.concatenate(tiles, axis=0).astype(jnp.bfloat16)

    for d in range(8):

        @pl.when(jnp.logical_not(jnp.logical_and(mine, day == d)))
        def _():
            ref_copy(1, 0, d).wait_recv()

    summed = ref_recv[0].astype(jnp.float32)
    for d in range(1, 8):
        summed = summed + ref_recv[d].astype(jnp.float32)
    ref_wide[...] = summed

    def share(q):
        if q < 16:
            return ref_wide[pl.ds(q, 4, stride=16), :]
        return ref_wide[pl.ds(64 + q - 16, 4, stride=4), :]

    for half in range(2):
        factor = mask_own[0:4, :] / jnp.maximum(share(half * 10 + 9), 1.0)
        for p in range(9):
            stack_ref[p, 0, :, half * LANES : (half + 1) * LANES] = share(half * 10 + p) * factor

    for k in range(NC):
        for step in (1, 3):
            z_copy(step, k, own).wait_send()

        @pl.when(outer)
        def _():
            z_copy(2, k, own).wait_send()

        @pl.when(inner)
        def _():
            relay(k, own, z0).wait_send()

        for step in (1, 2, 3):
            x_copy(step, k, x0).wait_send()
        for step in range(4):
            core_copy(step, k, c0).wait_send()
    for step in (1, 2, 3):
        hour_copy(step, x0).wait_send()
        for h in range(2):
            ref_copy(step, h, day).wait_send()
    for h in range(2):

        @pl.when(jnp.logical_not(jnp.logical_and(mine, h0 == h)))
        def _():
            ref_copy(0, h, day).wait_send()


def on_device(spectra, flags, pair_mask):
    table = jnp.asarray(lag_table())
    bf16, f32 = jnp.bfloat16, jnp.float32
    dma = pltpu.SemaphoreType.DMA
    vmem = pltpu.VMEM
    operands = (jnp.transpose(spectra, (0, 1, 3, 2, 4)), flags, pair_mask, table)
    return pl.pallas_call(
        kernel,
        out_shape=(
            jax.ShapeDtypeStruct((1, 9, 1, 32, LAGS), bf16),
            jax.ShapeDtypeStruct((9, 1, 4, LAGS), f32),
        ),
        in_specs=[pl.BlockSpec(memory_space=pl.ANY)] * 4,
        out_specs=(
            pl.BlockSpec(memory_space=pltpu.VMEM),
            pl.BlockSpec(memory_space=pltpu.VMEM),
        ),
        scratch_shapes=[
            vmem((1, 2, 3, WIN, BINS), bf16),
            vmem((1, WIN), jnp.int32),
            vmem((1, 32), jnp.int32),
            vmem((8, BINS + PAD), f32),
            vmem((ROWS, LANES), f32),
            vmem((8, ROWS, LANES), bf16),
            vmem((4, ROWS, LANES), bf16),
            vmem((8 * ROWS, LANES), f32),
            vmem((4 * ROWS, LANES), f32),
            vmem((2 * BINS, LAGS), bf16),
            vmem((288, 2 * BINS), bf16),
            vmem((288, LAGS), f32),
            vmem((32, LANES), f32),
            vmem((8, LANES), f32),
            vmem((4 * 160, LANES), f32),
            vmem((4, 160, LANES), bf16),
            vmem((4, 160, LANES), bf16),
            vmem((4, 2, 80, LANES), bf16),
            vmem((8, 80, LANES), bf16),
            vmem((80, LANES), f32),
            dma((3,)),
            dma,
            dma((4, NC)),
            dma((4, NC)),
            dma((NC,)),
            dma((4, NC)),
            dma((4, NC)),
            dma((4, NC)),
            dma((4, NC)),
            dma((4,)),
            dma((4,)),
            dma((4, 2)),
            dma((8,)),
            pltpu.SemaphoreType.REGULAR,
        ],
        compiler_params=pltpu.CompilerParams(
            collective_id=0, has_side_effects=True, vmem_limit_bytes=32 * 1024 * 1024
        ),
        cost_estimate=pl.CostEstimate(
            flops=500_000_000, bytes_accessed=2_000_000, transcendentals=6144
        ),
    )(*(pltpu.with_memory_space_constraint(a, pltpu.HBM) for a in operands))


def solution(mesh):
    placed = (P("sta", None, "day", None, None), P("sta", "day"), P("sta", None))
    return jax.shard_map(
        on_device,
        mesh=mesh,
        in_specs=placed,
        out_specs=(P("day", None, "sta", None, None), P(None, "sta", "day", None)),
        check_vma=False,
    )
```

time: 37.5 us -> 32.4 us (0.86)
  local copies, waits for them, and re-layouts: 4.92 us -> 1.28 us
  Pallas kernels: 31.7 us -> 30.4 us
    unnamed x9 -> x2, local copies, waits for them, and re-layouts: 4.92 us -> 1.28 us
    pallas_call x1, Pallas kernels: 31.7 us -> 30.4 us  [on_device(): pl.pallas_call(kernel, out_shape=(jax.ShapeDtypeStruct((1, 9, 1, 32, LAGS...]
where the time goes in v2:
time: 32.4 us; the launch traced here: 32.3 us
  Pallas kernels  30.4 us (94%)
  local copies, waits for them, and re-layouts  1.28 us (4%)
  between operations  0.64 us (2%)
    pallas_call x1, Pallas kernels, on_device(): pl.pallas_call(kernel, out_shape=(jax.ShapeDtypeStruct((1, 9, 1, 32, LAGS...  30.4 us
    unnamed x2, local copies, waits for them, and re-layouts  1.28 us

profile of v2, /device:TPU:1, one launch (start us, length us, event | category | flops | bytes accessed | tf_op | source)
XLA Modules:
  0.0 32.3 jit_solution(16966305112933077989)
XLA Ops:
  0.6 30.4 %shard_map.59 = (bf16[1,9,1,32,256]{4,3,2,1,0:T(8,128)(2,1)S(1)}, f32[9,1,4,256]{3,2,1,0:T(4,128)S(1)}) custom-call(bf16[1,2,3,4,1536]{4,3,2,1,0:T(4,128)(2,1)} %bitcast.1, s32[1,4]{1,0:T(1,128)} %flags_hbm.1, s32[1,32]{1,0:T(1,128)} %mask_hbm.1, bf16[3072,256]{1,0:T(8,128)(2,1)} %constant.2.clone.table_hbm), custom_call_target="tpu_custom_call" | custom-call | flops 500000000 | bytes 2000000 | tf_op jit(solution)/shard_map/pallas_call | solution.py:450
  31.1 0.7 %copy.8 = bf16[1,9,1,32,256]{4,3,2,1,0:T(8,128)(2,1)} copy(bf16[1,9,1,32,256]{4,3,2,1,0:T(8,128)(2,1)S(1)} %get-tuple-element.4) | data formatting | bytes 294912
  31.7 0.6 %copy.9 = f32[9,1,4,256]{3,2,1,0:T(4,128)} copy(f32[9,1,4,256]{3,2,1,0:T(4,128)S(1)} %get-tuple-element.5) | data formatting | bytes 73728

commit v3 on v2

v3 whole, which is shorter than its diff:
```python
import math

import jax
import jax.numpy as jnp
import ml_dtypes
import numpy as np
from jax import lax
from jax.experimental import pallas as pl
from jax.experimental.pallas import tpu as pltpu
from jax.sharding import PartitionSpec as P

BINS = 1536
LAGS = 256
HALF_BAND = 16
WIN = 4
LANES = 128
FC = BINS // LANES
ROWS_FC = 24
FLAG_ROWS = 16
ROWS = FLAG_ROWS + FC * ROWS_FC
BLOCK = 80
PAD = 128
MESH = pl.DeviceIdType.MESH


def lag_table():
    freq = np.arange(BINS, dtype=np.int64)
    lag = np.arange(LAGS, dtype=np.int64) - LAGS // 2
    angle = (freq[:, None] * lag[None, :] % (2 * BINS)) * (math.pi / BINS)
    parts = np.stack([np.cos(angle), -np.sin(angle)]).reshape(2, FC, LANES, LAGS)
    rows = np.transpose(parts, (1, 0, 2, 3)).reshape(2 * BINS, LAGS)
    return rows.astype(np.float32).astype(ml_dtypes.bfloat16)


def kernel(
    spec_hbm, flags_hbm, mask_hbm, table_hbm,
    hourly_ref, stack_ref,
    spec_ref, flags_ref, mask_ref, power, white, t_blocks, s_blocks, t_wide, s_wide, table, products, totals,
    mask_col, mask_own, result, hour_recv, ref_recv, hour_wide, hour_rest, ref_wide,
    in_sems, table_sem, zs, zr, fs, xs, xr, cs, cr, hs, hr, rs, rr, ready,
):
    sta = lax.axis_index("sta")
    day = lax.axis_index("day")
    x0, z0, c0 = sta // 8, (sta // 2) % 4, sta % 2
    y0, h0 = day // 2, day % 2

    def sta_of(x, z, c):
        return (x * 4 + z) * 2 + c

    def at(x, z, c, d):
        return (sta_of(x, z, c), d)

    sibling = at(x0, z0, 1 - c0, day)

    barrier = pltpu.get_barrier_semaphore()

    def greet(target):
        pl.semaphore_signal(barrier, inc=1, device_id=target, device_id_type=MESH)

    for step in (3, 1, 2):
        greet(at(x0, (z0 + step) % 4, c0, day))
    for step in (2, 1, 3):
        greet(at((x0 + step) % 4, z0, c0, day))
    greet(sibling)
    mine = x0 == y0
    early = h0 == 0
    for y in range(4):

        @pl.when(y != y0)
        def _():
            greet(at(x0, z0, c0, y * 2 + h0))

        @pl.when(early)
        def _():
            greet(at(y0, z0, c0, y * 2 + 1))
            greet(at(y, z0, c0, x0 * 2 + 1))

    loads = [
        pltpu.make_async_copy(spec_hbm, spec_ref, in_sems.at[0]),
        pltpu.make_async_copy(flags_hbm, flags_ref, in_sems.at[1]),
        pltpu.make_async_copy(mask_hbm, mask_ref, in_sems.at[2]),
    ]
    for load in loads:
        load.start()
    table_copy = pltpu.make_async_copy(table_hbm, table, table_sem)
    table_copy.start()

    loads[0].wait()
    loads[1].wait()
    power[...] = jnp.zeros_like(power)
    energy = None
    for part in range(2):
        for comp in range(3):
            values = spec_ref[0, part, comp].astype(jnp.float32)
            energy = values * values if energy is None else energy + values * values
    power[0:WIN, 0:BINS] = energy
    single = power[...]
    span = single
    for shift in (1, 2, 4, 8, 16):
        span = span + pltpu.roll(span, shift, axis=1)
    span = span + pltpu.roll(single, 2 * HALF_BAND, axis=1)
    smooth = pltpu.roll(span, BINS + PAD - HALF_BAND, axis=1)[0:WIN, 0:BINS]
    line = lax.broadcasted_iota(jnp.int32, (WIN, WIN), 0)
    place = lax.broadcasted_iota(jnp.int32, (WIN, WIN), 1)
    spread = jnp.broadcast_to((1 - flags_ref[...]).astype(jnp.float32), (WIN, WIN))
    good = jnp.sum(jnp.where(line == place, spread, 0.0), axis=1, keepdims=True)
    scale = lax.rsqrt(smooth / (6.0 * (2 * HALF_BAND + 1)) + 1e-06) * good
    for part in range(2):
        for comp in range(3):
            y = spec_ref[0, part, comp].astype(jnp.float32) * scale
            first = FLAG_ROWS + (part * 3 + comp) * WIN
            for fc in range(FC):
                white[first + fc * ROWS_FC : first + fc * ROWS_FC + WIN, :] = y[
                    :, fc * LANES : (fc + 1) * LANES
                ]
    white[0:WIN, :] = jnp.broadcast_to(good, (WIN, LANES))
    white[WIN:FLAG_ROWS, :] = jnp.zeros((FLAG_ROWS - WIN, LANES), jnp.float32)
    block = white[...].astype(jnp.bfloat16)
    own = z0 * 2 + c0
    t_blocks[own] = block
    s_blocks[x0] = block

    loads[2].wait()
    spread = jnp.broadcast_to(mask_ref[...].astype(jnp.float32), (32, 32))
    line = lax.broadcasted_iota(jnp.int32, (32, 32), 0)
    place = lax.broadcasted_iota(jnp.int32, (32, 32), 1)
    column = jnp.sum(jnp.where(line == place, spread, 0.0), axis=1, keepdims=True)
    mask_col[...] = jnp.broadcast_to(column, (32, LANES))
    column = jnp.sum(
        jnp.where(line[0:8] + day * 4 == place[0:8], spread[0:8], 0.0), axis=1, keepdims=True
    )
    mask_own[...] = jnp.broadcast_to(column, (8, LANES))

    @pl.when(early)
    def _():
        pl.semaphore_wait(barrier, 10)

    @pl.when(jnp.logical_not(early))
    def _():
        pl.semaphore_wait(barrier, 18)
        for y in range(4):
            pl.semaphore_signal(
                ready, inc=1, device_id=at(y0, z0, c0, y * 2), device_id_type=MESH
            )


    def z_copy(step, slot):
        return pltpu.make_async_remote_copy(
            src_ref=t_blocks.at[own],
            dst_ref=t_blocks.at[slot],
            send_sem=zs.at[step],
            recv_sem=zr.at[step],
            device_id=at(x0, (z0 + step) % 4, c0, day),
            device_id_type=MESH,
        )

    def relay(slot, z):
        return pltpu.make_async_remote_copy(
            src_ref=t_blocks.at[slot],
            dst_ref=t_blocks.at[slot],
            send_sem=fs,
            recv_sem=zr.at[2],
            device_id=at(x0, z, c0, day),
            device_id_type=MESH,
        )

    def x_copy(step, slot):
        return pltpu.make_async_remote_copy(
            src_ref=s_blocks.at[x0],
            dst_ref=s_blocks.at[slot],
            send_sem=xs.at[step],
            recv_sem=xr.at[step],
            device_id=at((x0 + step) % 4, z0, c0, day),
            device_id_type=MESH,
        )

    order = [z0, 1 + z0 % 2, 3 * (1 - z0 % 2), (z0 + 2) % 4]

    def core_copy(i, core):
        slot = order[i] * 2 + core
        return pltpu.make_async_remote_copy(
            src_ref=t_blocks.at[slot],
            dst_ref=t_blocks.at[slot],
            send_sem=cs.at[i],
            recv_sem=cr.at[i],
            device_id=sibling,
            device_id_type=MESH,
        )

    outer = jnp.logical_or(z0 == 0, z0 == 3)
    inner = jnp.logical_not(outer)

    @pl.when(z0 >= 2)
    def _():
        z_copy(1, own).start()
        z_copy(3, own).start()

    @pl.when(z0 < 2)
    def _():
        z_copy(3, own).start()
        z_copy(1, own).start()

    @pl.when(outer)
    def _():
        z_copy(2, own).start()

    for step in (2, 1, 3):
        x_copy(step, x0).start()
    core_copy(0, c0).start()

    def arrive(i):
        slot = order[i] * 2 + c0
        z_copy((z0 - order[i] + 4) % 4, slot).wait_recv()
        if i == 1:

            @pl.when(inner)
            def _():
                relay(slot, 3 * (z0 - 1)).start()

        core_copy(i, c0).start()

    high_rows = lax.broadcasted_iota(jnp.int32, (8, LANES), 0) >= 4

    def t_tile(row):
        first = jnp.broadcast_to(t_wide[pl.ds(row, 1), :], (8, LANES))
        second = jnp.broadcast_to(t_wide[pl.ds(ROWS + row, 1), :], (8, LANES))
        return jnp.where(high_rows, second, first)

    def s_tile(row):
        return s_wide[pl.ds(row, 8, stride=ROWS), :]

    def cross(i):
        for core in range(2):
            t_wide[core * ROWS : (core + 1) * ROWS, :] = t_blocks[order[i] * 2 + core].astype(
                jnp.float32
            )

        def chunk(fc, carry):
            base = FLAG_ROWS + fc * ROWS_FC
            local = [s_tile(base + r) for r in range(ROWS_FC)]
            column = pl.multiple_of(fc * 2 * LANES, 2 * LANES)
            re_tiles, im_tiles = [None] * 9, [None] * 9
            for b in range(3):
                other = [
                    t_tile(base + (part * 3 + b) * WIN + w) for part in range(2) for w in range(WIN)
                ]
                for a in range(3):
                    re, im = None, None
                    for w in range(WIN):
                        s_re, s_im = local[a * WIN + w], local[(3 + a) * WIN + w]
                        t_re, t_im = other[w], other[WIN + w]
                        re_term = s_re * t_re + s_im * t_im
                        im_term = s_im * t_re - s_re * t_im
                        re = re_term if re is None else re + re_term
                        im = im_term if im is None else im + im_term
                    re_tiles[a * 3 + b] = re
                    im_tiles[a * 3 + b] = im
            rows = pl.ds(i * BLOCK, BLOCK)
            zero = jnp.zeros((8, LANES), jnp.float32)
            products[rows, pl.ds(column, LANES)] = jnp.concatenate(
                re_tiles + [zero], axis=0
            ).astype(jnp.bfloat16)
            products[rows, pl.ds(column + LANES, LANES)] = jnp.concatenate(
                im_tiles + [zero], axis=0
            ).astype(jnp.bfloat16)
            return carry

        lax.fori_loop(0, FC, chunk, 0)
        count = None
        for w in range(WIN):
            g = s_tile(w) * t_tile(w)
            count = g if count is None else count + g
        for half in range(2):
            totals[pl.ds(half * 4 * BLOCK + order[i] * BLOCK + 72, 8), :] = count

    def transform(low, high):
        term = jnp.dot(
            products[low * BLOCK : high * BLOCK, :], table[...], preferred_element_type=jnp.float32
        ) * (1.0 / math.sqrt(BINS))
        for i in range(low, high):
            for half in range(2):
                rows = pl.ds(pl.multiple_of(half * 4 * BLOCK + order[i] * BLOCK, 8), 72)
                totals[rows, :] = term[
                    (i - low) * BLOCK : (i - low) * BLOCK + 72, half * LANES : (half + 1) * LANES
                ]

    arrive(1)
    for step in (1, 3, 2):
        x_copy(step, (x0 - step + 4) % 4).wait_recv()
    for slot in range(4):
        values = s_blocks[slot].astype(jnp.float32)
        s_wide[slot * ROWS : (slot + 1) * ROWS, :] = values
        s_wide[(4 + slot) * ROWS : (5 + slot) * ROWS, :] = values
    core_copy(0, 1 - c0).wait_recv()
    cross(0)
    arrive(2)
    core_copy(1, 1 - c0).wait_recv()
    cross(1)
    arrive(3)
    core_copy(2, 1 - c0).wait_recv()
    cross(2)
    table_copy.wait()
    transform(0, 3)
    core_copy(3, 1 - c0).wait_recv()
    cross(3)
    transform(3, 4)

    def hour_copy(step, slot):
        return pltpu.make_async_remote_copy(
            src_ref=result.at[step],
            dst_ref=hour_recv.at[slot],
            send_sem=hs.at[step],
            recv_sem=hr.at[step],
            device_id=at((x0 + step) % 4, z0, c0, day),
            device_id_type=MESH,
        )

    def ref_copy(step, h, slot):
        return pltpu.make_async_remote_copy(
            src_ref=result.at[step, h],
            dst_ref=ref_recv.at[slot],
            send_sem=rs.at[step, h],
            recv_sem=rr.at[slot],
            device_id=at((x0 + step) % 4, z0, c0, x0 * 2 + h),
            device_id_type=MESH,
        )

    for h in range(2):
        for step in (2, 1, 3, 0):
            x = (x0 + step) % 4
            starts = [
                half * 4 * BLOCK + (2 * h + bit) * BLOCK + core * 4 + x
                for bit in range(2)
                for core in range(2)
                for half in range(2)
            ]
            tiles = [totals[pl.ds(first, 8, stride=8), :] for first in starts]
            rest = [totals[pl.ds(first + 64, 2, stride=8), :] for first in starts]
            result[step, h] = jnp.concatenate(tiles + rest, axis=0).astype(jnp.bfloat16)
            if h == 0:

                @pl.when(jnp.logical_not(early))
                def _():
                    ref_copy(step, 0, day).start()

    def send_ref(step, h):
        if step:
            ref_copy(step, h, day).start()
        else:
            local = jnp.logical_and(mine, h0 == h)

            @pl.when(local)
            def _():
                ref_recv[day] = result[0, h]

            @pl.when(jnp.logical_not(local))
            def _():
                ref_copy(0, h, day).start()

    @pl.when(early)
    def _():
        for step in (2, 1, 3, 0):
            send_ref(step, 0)

    @pl.when(jnp.logical_not(early))
    def _():
        for step in (2, 1, 3, 0):
            send_ref(step, 1)

    for step in (2, 1, 3):
        hour_copy(step, x0).start()
    hour_recv[x0] = result[0]

    @pl.when(early)
    def _():
        pl.semaphore_wait(ready, 4)
        for step in (2, 1, 3, 0):
            ref_copy(step, 1, day).start()

    for step in (1, 3, 2):
        hour_copy(step, (x0 - step + 4) % 4).wait_recv()
    for x in range(4):
        for h in range(2):
            got = hour_recv[x, h].astype(jnp.float32)
            hour_wide[x * 128 + h * 64 : x * 128 + h * 64 + 64, :] = got[0:64]
            hour_rest[x * 32 + h * 16 : x * 32 + h * 16 + 16, :] = got[64:80]

    def hour_tile(x, half, p):
        if p < 8:
            return hour_wide[pl.ds(x * 128 + half * 8 + p, 8, stride=16), :]
        return hour_rest[pl.ds(x * 32 + half * 2 + p - 8, 8, stride=4), :]

    for pair in range(2):
        for half in range(2):
            factors = [
                mask_col[x * 8 : x * 8 + 8, :] / jnp.maximum(hour_tile(x, half, 9), 1.0)
                for x in (pair * 2, pair * 2 + 1)
            ]
            for p in range(9):
                tiles = [hour_tile(pair * 2 + i, half, p) * factors[i] for i in range(2)]
                hourly_ref[
                    0, p, 0, pair * 16 : pair * 16 + 16, half * LANES : (half + 1) * LANES
                ] = jnp.concatenate(tiles, axis=0).astype(jnp.bfloat16)

    for d in range(8):

        @pl.when(jnp.logical_not(jnp.logical_and(mine, day == d)))
        def _():
            ref_copy(1, 0, d).wait_recv()

    summed = ref_recv[0].astype(jnp.float32)
    for d in range(1, 8):
        summed = summed + ref_recv[d].astype(jnp.float32)
    ref_wide[...] = summed

    def share(half, p):
        if p < 8:
            return ref_wide[pl.ds(half * 8 + p, 4, stride=16), :]
        return ref_wide[pl.ds(64 + half * 2 + p - 8, 4, stride=4), :]

    for half in range(2):
        factor = mask_own[0:4, :] / jnp.maximum(share(half, 9), 1.0)
        for p in range(9):
            stack_ref[p, 0, :, half * LANES : (half + 1) * LANES] = share(half, p) * factor

    for step in (1, 3):
        z_copy(step, own).wait_send()

    @pl.when(outer)
    def _():
        z_copy(2, own).wait_send()

    @pl.when(inner)
    def _():
        relay(own, z0).wait_send()

    for step in (1, 2, 3):
        x_copy(step, x0).wait_send()
        hour_copy(step, x0).wait_send()
        for h in range(2):
            ref_copy(step, h, day).wait_send()
    for i in range(4):
        core_copy(i, c0).wait_send()
    for h in range(2):

        @pl.when(jnp.logical_not(jnp.logical_and(mine, h0 == h)))
        def _():
            ref_copy(0, h, day).wait_send()


def on_device(spectra, flags, pair_mask):
    table = jnp.asarray(lag_table())
    bf16, f32 = jnp.bfloat16, jnp.float32
    dma = pltpu.SemaphoreType.DMA
    vmem = pltpu.VMEM
    operands = (jnp.transpose(spectra, (0, 1, 3, 2, 4)), flags, pair_mask, table)
    return pl.pallas_call(
        kernel,
        out_shape=(
            jax.ShapeDtypeStruct((1, 9, 1, 32, LAGS), bf16),
            jax.ShapeDtypeStruct((9, 1, 4, LAGS), f32),
        ),
        in_specs=[pl.BlockSpec(memory_space=pl.ANY)] * 4,
        out_specs=(
            pl.BlockSpec(memory_space=pltpu.VMEM),
            pl.BlockSpec(memory_space=pltpu.VMEM),
        ),
        scratch_shapes=[
            vmem((1, 2, 3, WIN, BINS), bf16),
            vmem((1, WIN), jnp.int32),
            vmem((1, 32), jnp.int32),
            vmem((8, BINS + PAD), f32),
            vmem((ROWS, LANES), f32),
            vmem((8, ROWS, LANES), bf16),
            vmem((4, ROWS, LANES), bf16),
            vmem((2 * ROWS, LANES), f32),
            vmem((8 * ROWS, LANES), f32),
            vmem((2 * BINS, LAGS), bf16),
            vmem((4 * BLOCK, 2 * BINS), bf16),
            vmem((8 * BLOCK, LANES), f32),
            vmem((32, LANES), f32),
            vmem((8, LANES), f32),
            vmem((4, 2, BLOCK, LANES), bf16),
            vmem((4, 2, BLOCK, LANES), bf16),
            vmem((8, BLOCK, LANES), bf16),
            vmem((4 * 128, LANES), f32),
            vmem((4 * 32, LANES), f32),
            vmem((BLOCK, LANES), f32),
            dma((3,)),
            dma,
            dma((4,)),
            dma((4,)),
            dma,
            dma((4,)),
            dma((4,)),
            dma((4,)),
            dma((4,)),
            dma((4,)),
            dma((4,)),
            dma((4, 2)),
            dma((8,)),
            pltpu.SemaphoreType.REGULAR,
        ],
        compiler_params=pltpu.CompilerParams(
            collective_id=0, has_side_effects=True, vmem_limit_bytes=32 * 1024 * 1024
        ),
        cost_estimate=pl.CostEstimate(
            flops=500_000_000, bytes_accessed=2_000_000, transcendentals=6144
        ),
    )(*(pltpu.with_memory_space_constraint(a, pltpu.HBM) for a in operands))


def solution(mesh):
    placed = (P("sta", None, "day", None, None), P("sta", "day"), P("sta", None))
    return jax.shard_map(
        on_device,
        mesh=mesh,
        in_specs=placed,
        out_specs=(P("day", None, "sta", None, None), P(None, "sta", "day", None)),
        check_vma=False,
    )
```

time: 32.4 us -> 30.6 us (0.944)
  Pallas kernels: 30.4 us -> 28.5 us
    pallas_call x1, Pallas kernels: 30.4 us -> 28.5 us  [on_device(): pl.pallas_call(kernel, out_shape=(jax.ShapeDtypeStruct((1, 9, 1, 32, LAGS...]
where the time goes in v3:
time: 30.6 us; the launch traced here: 30.4 us
  Pallas kernels  28.5 us (93%)
  local copies, waits for them, and re-layouts  1.28 us (4%)
  between operations  0.64 us (2%)
    pallas_call x1, Pallas kernels, on_device(): pl.pallas_call(kernel, out_shape=(jax.ShapeDtypeStruct((1, 9, 1, 32, LAGS...  28.5 us
    unnamed x2, local copies, waits for them, and re-layouts  1.28 us

profile of v3, /device:TPU:1, one launch (start us, length us, event | category | flops | bytes accessed | tf_op | source)
XLA Modules:
  0.0 30.4 jit_solution(15179994417306561967)
XLA Ops:
  0.6 28.5 %shard_map.59 = (bf16[1,9,1,32,256]{4,3,2,1,0:T(8,128)(2,1)S(1)}, f32[9,1,4,256]{3,2,1,0:T(4,128)S(1)}) custom-call(bf16[1,2,3,4,1536]{4,3,2,1,0:T(4,128)(2,1)} %bitcast.1, s32[1,4]{1,0:T(1,128)} %flags_hbm.1, s32[1,32]{1,0:T(1,128)} %mask_hbm.1, bf16[3072,256]{1,0:T(8,128)(2,1)} %constant.2.clone.table_hbm), custom_call_target="tpu_custom_call" | custom-call | flops 500000000 | bytes 2000000 | tf_op jit(solution)/shard_map/pallas_call | solution.py:457
  29.1 0.7 %copy.8 = bf16[1,9,1,32,256]{4,3,2,1,0:T(8,128)(2,1)} copy(bf16[1,9,1,32,256]{4,3,2,1,0:T(8,128)(2,1)S(1)} %get-tuple-element.4) | data formatting | bytes 294912
  29.8 0.6 %copy.9 = f32[9,1,4,256]{3,2,1,0:T(4,128)} copy(f32[9,1,4,256]{3,2,1,0:T(4,128)S(1)} %get-tuple-element.5) | data formatting | bytes 73728

commit v4 on v3

--- a/solution.py
+++ b/solution.py
@@ -35,7 +35,7 @@
 def kernel(
     spec_hbm, flags_hbm, mask_hbm, table_hbm,
     hourly_ref, stack_ref,
-    spec_ref, flags_ref, mask_ref, power, white, t_blocks, s_blocks, t_wide, s_wide, table, products, totals,
+    spec_ref, flags_ref, mask_ref, power, white, t_blocks, s_blocks, t_wide, s_wide, s_tiles, table, products, totals,
     mask_col, mask_own, result, hour_recv, ref_recv, hour_wide, hour_rest, ref_wide,
     in_sems, table_sem, zs, zr, fs, xs, xr, cs, cr, hs, hr, rs, rr, ready,
 ):
@@ -174,7 +174,7 @@
             device_id_type=MESH,
         )
 
-    order = [z0, 1 + z0 % 2, 3 * (1 - z0 % 2), (z0 + 2) % 4]
+    order = [z0, z0 + 1 - 2 * (z0 % 2), 3 - z0, (z0 + 2) % 4]
 
     def core_copy(i, core):
         slot = order[i] * 2 + core
@@ -190,33 +190,28 @@
     outer = jnp.logical_or(z0 == 0, z0 == 3)
     inner = jnp.logical_not(outer)
 
-    @pl.when(z0 >= 2)
+    @pl.when(z0 % 2 == 0)
     def _():
         z_copy(1, own).start()
         z_copy(3, own).start()
 
-    @pl.when(z0 < 2)
+    @pl.when(z0 % 2 == 1)
     def _():
         z_copy(3, own).start()
         z_copy(1, own).start()
 
-    @pl.when(outer)
-    def _():
-        z_copy(2, own).start()
-
     for step in (2, 1, 3):
         x_copy(step, x0).start()
+
+    @pl.when(outer)
+    def _():
+        z_copy(2, own).start()
+
     core_copy(0, c0).start()
 
     def arrive(i):
         slot = order[i] * 2 + c0
         z_copy((z0 - order[i] + 4) % 4, slot).wait_recv()
-        if i == 1:
-
-            @pl.when(inner)
-            def _():
-                relay(slot, 3 * (z0 - 1)).start()
-
         core_copy(i, c0).start()
 
     high_rows = lax.broadcasted_iota(jnp.int32, (8, LANES), 0) >= 4
@@ -227,7 +222,7 @@
         return jnp.where(high_rows, second, first)
 
     def s_tile(row):
-        return s_wide[pl.ds(row, 8, stride=ROWS), :]
+        return s_tiles[pl.ds(pl.multiple_of(row * 8, 8), 8), :]
 
     def cross(i):
         for core in range(2):
@@ -284,27 +279,6 @@
                     (i - low) * BLOCK : (i - low) * BLOCK + 72, half * LANES : (half + 1) * LANES
                 ]
 
-    arrive(1)
-    for step in (1, 3, 2):
-        x_copy(step, (x0 - step + 4) % 4).wait_recv()
-    for slot in range(4):
-        values = s_blocks[slot].astype(jnp.float32)
-        s_wide[slot * ROWS : (slot + 1) * ROWS, :] = values
-        s_wide[(4 + slot) * ROWS : (5 + slot) * ROWS, :] = values
-    core_copy(0, 1 - c0).wait_recv()
-    cross(0)
-    arrive(2)
-    core_copy(1, 1 - c0).wait_recv()
-    cross(1)
-    arrive(3)
-    core_copy(2, 1 - c0).wait_recv()
-    cross(2)
-    table_copy.wait()
-    transform(0, 3)
-    core_copy(3, 1 - c0).wait_recv()
-    cross(3)
-    transform(3, 4)
-
     def hour_copy(step, slot):
         return pltpu.make_async_remote_copy(
             src_ref=result.at[step],
@@ -325,7 +299,7 @@
             device_id_type=MESH,
         )
 
-    for h in range(2):
+    def send_share(h):
         for step in (2, 1, 3, 0):
             x = (x0 + step) % 4
             starts = [
@@ -337,35 +311,70 @@
             tiles = [totals[pl.ds(first, 8, stride=8), :] for first in starts]
             rest = [totals[pl.ds(first + 64, 2, stride=8), :] for first in starts]
             result[step, h] = jnp.concatenate(tiles + rest, axis=0).astype(jnp.bfloat16)
-            if h == 0:
-
-                @pl.when(jnp.logical_not(early))
+            now = jnp.logical_or(jnp.logical_not(early), h == 0)
+            if step == 0:
+                local = jnp.logical_and(mine, h0 == h)
+
+                @pl.when(local)
                 def _():
-                    ref_copy(step, 0, day).start()
-
-    def send_ref(step, h):
-        if step:
-            ref_copy(step, h, day).start()
-        else:
-            local = jnp.logical_and(mine, h0 == h)
-
-            @pl.when(local)
+                    ref_recv[day] = result[0, h]
+
+                now = jnp.logical_and(now, jnp.logical_not(local))
+
+            @pl.when(now)
             def _():
-                ref_recv[day] = result[0, h]
-
-            @pl.when(jnp.logical_not(local))
-            def _():
-                ref_copy(0, h, day).start()
-
-    @pl.when(early)
-    def _():
-        for step in (2, 1, 3, 0):
-            send_ref(step, 0)
-
-    @pl.when(jnp.logical_not(early))
-    def _():
-        for step in (2, 1, 3, 0):
-            send_ref(step, 1)
+                ref_copy(step, h, day).start()
+
+    arrive(1)
+
+    @pl.when(inner)
+    def _():
+        arrive(2)
+        relay(order[2] * 2 + c0, 3 * (z0 - 1)).start()
+
+    for step in (1, 3, 2):
+        x_copy(step, (x0 - step + 4) % 4).wait_recv()
+    for slot in range(4):
+        values = s_blocks[slot].astype(jnp.float32)
+        s_wide[slot * ROWS : (slot + 1) * ROWS, :] = values
+        s_wide[(4 + slot) * ROWS : (5 + slot) * ROWS, :] = values
+
+    def prepare(i, carry):
+        for r in range(16):
+            row = i * 16 + r
+            s_tiles[pl.ds(pl.multiple_of(row * 8, 8), 8), :] = s_wide[
+                pl.ds(row, 8, stride=ROWS), :
+            ]
+        return carry
+
+    lax.fori_loop(0, ROWS // 16, prepare, 0)
+    core_copy(0, 1 - c0).wait_recv()
+    cross(0)
+    core_copy(1, 1 - c0).wait_recv()
+    cross(1)
+    table_copy.wait()
+
+    @pl.when(z0 < 2)
+    def _():
+        transform(0, 2)
+        send_share(z0 // 2)
+
+    @pl.when(outer)
+    def _():
+        arrive(2)
+
+    core_copy(2, 1 - c0).wait_recv()
+    cross(2)
+    arrive(3)
+    core_copy(3, 1 - c0).wait_recv()
+    cross(3)
+    transform(2, 4)
+    send_share(1 - z0 // 2)
+
+    @pl.when(z0 >= 2)
+    def _():
+        transform(0, 2)
+        send_share(z0 // 2)
 
     for step in (2, 1, 3):
         hour_copy(step, x0).start()
@@ -448,18 +457,30 @@
             ref_copy(0, h, day).wait_send()
 
 
+def write_out(hourly_ref, stack_ref, hourly_hbm, stack_hbm, sems):
+    copies = [
+        pltpu.make_async_copy(hourly_ref, hourly_hbm, sems.at[0]),
+        pltpu.make_async_copy(stack_ref, stack_hbm, sems.at[1]),
+    ]
+    for copy in copies:
+        copy.start()
+    for copy in copies:
+        copy.wait()
+
+
 def on_device(spectra, flags, pair_mask):
     table = jnp.asarray(lag_table())
     bf16, f32 = jnp.bfloat16, jnp.float32
     dma = pltpu.SemaphoreType.DMA
     vmem = pltpu.VMEM
     operands = (jnp.transpose(spectra, (0, 1, 3, 2, 4)), flags, pair_mask, table)
-    return pl.pallas_call(
+    shapes = (
+        jax.ShapeDtypeStruct((1, 9, 1, 32, LAGS), bf16),
+        jax.ShapeDtypeStruct((9, 1, 4, LAGS), f32),
+    )
+    results = pl.pallas_call(
         kernel,
-        out_shape=(
-            jax.ShapeDtypeStruct((1, 9, 1, 32, LAGS), bf16),
-            jax.ShapeDtypeStruct((9, 1, 4, LAGS), f32),
-        ),
+        out_shape=shapes,
         in_specs=[pl.BlockSpec(memory_space=pl.ANY)] * 4,
         out_specs=(
             pl.BlockSpec(memory_space=pltpu.VMEM),
@@ -475,6 +496,7 @@
             vmem((4, ROWS, LANES), bf16),
             vmem((2 * ROWS, LANES), f32),
             vmem((8 * ROWS, LANES), f32),
+            vmem((8 * ROWS, LANES), f32),
             vmem((2 * BINS, LAGS), bf16),
             vmem((4 * BLOCK, 2 * BINS), bf16),
             vmem((8 * BLOCK, LANES), f32),
@@ -508,6 +530,14 @@
             flops=500_000_000, bytes_accessed=2_000_000, transcendentals=6144
         ),
     )(*(pltpu.with_memory_space_constraint(a, pltpu.HBM) for a in operands))
+    return pl.pallas_call(
+        write_out,
+        out_shape=shapes,
+        in_specs=[pl.BlockSpec(memory_space=pltpu.VMEM)] * 2,
+        out_specs=(pl.BlockSpec(memory_space=pl.ANY),) * 2,
+        scratch_shapes=[dma((2,))],
+        compiler_params=pltpu.CompilerParams(vmem_limit_bytes=1024 * 1024),
+    )(*results)
 
 
 def solution(mesh):

time: 30.6 us -> 27 us (0.88)
  the two profiles are of different devices: /device:TPU:1 before, /device:TPU:96 now
where the time goes in v4:
time: 27 us; the launch traced here: 26.9 us
  Pallas kernels  26.2 us (97%)
  between operations  0.64 us (2%)
    pallas_call x1, Pallas kernels, on_device(): pl.pallas_call(kernel, out_shape=shapes, in_specs=[pl.BlockSpec(memory_sp...  25.5 us
    pallas_call x1, Pallas kernels, on_device(): pl.pallas_call(write_out, out_shape=shapes, in_specs=[pl.BlockSpec(memory...  0.69 us

profile of v4, /device:TPU:96, one launch (start us, length us, event | category | flops | bytes accessed | tf_op | source)
XLA Modules:
  0.0 26.9 jit_solution(12679770111927025742)
XLA Ops:
  0.6 25.5 %shard_map.59 = (bf16[1,9,1,32,256]{4,3,2,1,0:T(8,128)(2,1)S(1)}, f32[9,1,4,256]{3,2,1,0:T(4,128)S(1)}) custom-call(bf16[1,2,3,4,1536]{4,3,2,1,0:T(4,128)(2,1)} %bitcast.1, s32[1,4]{1,0:T(1,128)} %flags_hbm.1, s32[1,32]{1,0:T(1,128)} %mask_hbm.1, bf16[3072,256]{1,0:T(8,128)(2,1)} %constant.2.clone.table_hbm), custom_call_target="tpu_custom_call" | custom-call | flops 500000000 | bytes 2000000 | tf_op jit(solution)/shard_map/pallas_call | solution.py:481
  26.2 0.7 %shard_map.60 = (bf16[1,9,1,32,256]{4,3,2,1,0:T(8,128)(2,1)}, f32[9,1,4,256]{3,2,1,0:T(4,128)}) custom-call(bf16[1,9,1,32,256]{4,3,2,1,0:T(8,128)(2,1)S(1)} %get-tuple-element.4.hourly_ref, f32[9,1,4,256]{3,2,1,0:T(4,128)S(1)} %get-tuple-element.5.stack_ref), custom_call_target="tpu_custom_call" | custom-call | tf_op jit(solution)/shard_map/pallas_call | solution.py:533

commit v5 on v4

--- a/solution.py
+++ b/solution.py
@@ -174,30 +174,27 @@
             device_id_type=MESH,
         )
 
-    order = [z0, z0 + 1 - 2 * (z0 % 2), 3 - z0, (z0 + 2) % 4]
-
-    def core_copy(i, core):
-        slot = order[i] * 2 + core
+    outer = jnp.logical_or(z0 == 0, z0 == 3)
+    inner = jnp.logical_not(outer)
+    def core_copy(z, core):
+        slot = z * 2 + core
         return pltpu.make_async_remote_copy(
             src_ref=t_blocks.at[slot],
             dst_ref=t_blocks.at[slot],
-            send_sem=cs.at[i],
-            recv_sem=cr.at[i],
+            send_sem=cs.at[z],
+            recv_sem=cr.at[z],
             device_id=sibling,
             device_id_type=MESH,
         )
 
-    outer = jnp.logical_or(z0 == 0, z0 == 3)
-    inner = jnp.logical_not(outer)
-
-    @pl.when(z0 % 2 == 0)
+    @pl.when(z0 == 0)
     def _():
         z_copy(1, own).start()
-        z_copy(3, own).start()
-
-    @pl.when(z0 % 2 == 1)
-    def _():
-        z_copy(3, own).start()
+
+    z_copy(3, own).start()
+
+    @pl.when(z0 > 0)
+    def _():
         z_copy(1, own).start()
 
     for step in (2, 1, 3):
@@ -207,12 +204,11 @@
     def _():
         z_copy(2, own).start()
 
-    core_copy(0, c0).start()
-
-    def arrive(i):
-        slot = order[i] * 2 + c0
-        z_copy((z0 - order[i] + 4) % 4, slot).wait_recv()
-        core_copy(i, c0).start()
+    core_copy(z0, c0).start()
+
+    def arrive(z):
+        z_copy((z0 - z + 4) % 4, z * 2 + c0).wait_recv()
+        core_copy(z, c0).start()
 
     high_rows = lax.broadcasted_iota(jnp.int32, (8, LANES), 0) >= 4
 
@@ -224,9 +220,9 @@
     def s_tile(row):
         return s_tiles[pl.ds(pl.multiple_of(row * 8, 8), 8), :]
 
-    def cross(i):
-        for core in range(2):
-            t_wide[core * ROWS : (core + 1) * ROWS, :] = t_blocks[order[i] * 2 + core].astype(
+    def cross(h, core):
+        for bit in range(2):
+            t_wide[bit * ROWS : (bit + 1) * ROWS, :] = t_blocks[(2 * h + bit) * 2 + core].astype(
                 jnp.float32
             )
 
@@ -250,7 +246,7 @@
                         im = im_term if im is None else im + im_term
                     re_tiles[a * 3 + b] = re
                     im_tiles[a * 3 + b] = im
-            rows = pl.ds(i * BLOCK, BLOCK)
+            rows = pl.ds(pl.multiple_of((2 * h + core) * BLOCK, 16), BLOCK)
             zero = jnp.zeros((8, LANES), jnp.float32)
             products[rows, pl.ds(column, LANES)] = jnp.concatenate(
                 re_tiles + [zero], axis=0
@@ -266,18 +262,18 @@
             g = s_tile(w) * t_tile(w)
             count = g if count is None else count + g
         for half in range(2):
-            totals[pl.ds(half * 4 * BLOCK + order[i] * BLOCK + 72, 8), :] = count
-
-    def transform(low, high):
+            first = (4 * half + 2 * h + core) * BLOCK + 72
+            totals[pl.ds(pl.multiple_of(first, 8), 8), :] = count
+
+    def transform(h, core):
         term = jnp.dot(
-            products[low * BLOCK : high * BLOCK, :], table[...], preferred_element_type=jnp.float32
+            products[pl.ds(pl.multiple_of((2 * h + core) * BLOCK, 16), BLOCK), :],
+            table[...],
+            preferred_element_type=jnp.float32,
         ) * (1.0 / math.sqrt(BINS))
-        for i in range(low, high):
-            for half in range(2):
-                rows = pl.ds(pl.multiple_of(half * 4 * BLOCK + order[i] * BLOCK, 8), 72)
-                totals[rows, :] = term[
-                    (i - low) * BLOCK : (i - low) * BLOCK + 72, half * LANES : (half + 1) * LANES
-                ]
+        for half in range(2):
+            first = pl.multiple_of((4 * half + 2 * h + core) * BLOCK, 8)
+            totals[pl.ds(first, 72), :] = term[0:72, half * LANES : (half + 1) * LANES]
 
     def hour_copy(step, slot):
         return pltpu.make_async_remote_copy(
@@ -289,48 +285,57 @@
             device_id_type=MESH,
         )
 
-    def ref_copy(step, h, slot):
+    def ref_copy(step, h, core, d):
+        slot = core * 8 + d
         return pltpu.make_async_remote_copy(
-            src_ref=result.at[step, h],
+            src_ref=result.at[step, core, h],
             dst_ref=ref_recv.at[slot],
-            send_sem=rs.at[step, h],
+            send_sem=rs.at[step, h, core],
             recv_sem=rr.at[slot],
             device_id=at((x0 + step) % 4, z0, c0, x0 * 2 + h),
             device_id_type=MESH,
         )
 
-    def send_share(h):
+    def send_share(h, core):
         for step in (2, 1, 3, 0):
             x = (x0 + step) % 4
             starts = [
-                half * 4 * BLOCK + (2 * h + bit) * BLOCK + core * 4 + x
+                (4 * half + 2 * h + core) * BLOCK + bit * 4 + x
                 for bit in range(2)
-                for core in range(2)
                 for half in range(2)
             ]
             tiles = [totals[pl.ds(first, 8, stride=8), :] for first in starts]
             rest = [totals[pl.ds(first + 64, 2, stride=8), :] for first in starts]
-            result[step, h] = jnp.concatenate(tiles + rest, axis=0).astype(jnp.bfloat16)
+            zero = jnp.zeros((8, LANES), jnp.float32)
+            result[step, core, h] = jnp.concatenate(tiles + rest + [zero], axis=0).astype(
+                jnp.bfloat16
+            )
             now = jnp.logical_or(jnp.logical_not(early), h == 0)
             if step == 0:
                 local = jnp.logical_and(mine, h0 == h)
 
                 @pl.when(local)
                 def _():
-                    ref_recv[day] = result[0, h]
+                    ref_recv[core * 8 + day] = result[0, core, h]
 
                 now = jnp.logical_and(now, jnp.logical_not(local))
 
             @pl.when(now)
             def _():
-                ref_copy(step, h, day).start()
-
-    arrive(1)
+                ref_copy(step, h, core, day).start()
+
+    @pl.when(outer)
+    def _():
+        arrive(1 + z0 // 3)
+
+    @pl.when(z0 == 1)
+    def _():
+        arrive(0)
 
     @pl.when(inner)
     def _():
-        arrive(2)
-        relay(order[2] * 2 + c0, 3 * (z0 - 1)).start()
+        arrive(3 - z0)
+        relay((3 - z0) * 2 + c0, 3 * (z0 - 1)).start()
 
     for step in (1, 3, 2):
         x_copy(step, (x0 - step + 4) % 4).wait_recv()
@@ -348,33 +353,47 @@
         return carry
 
     lax.fori_loop(0, ROWS // 16, prepare, 0)
+    def part(h, core):
+        cross(h, core)
+        transform(h, core)
+        send_share(h, core)
+
+    table_copy.wait()
+
+    @pl.when(z0 == 3)
+    def _():
+        cross(1, c0)
+
+    @pl.when(z0 >= 2)
+    def _():
+        arrive(0)
+
+    @pl.when(z0 == 3)
+    def _():
+        arrive(1)
+
+    part(0, c0)
     core_copy(0, 1 - c0).wait_recv()
-    cross(0)
     core_copy(1, 1 - c0).wait_recv()
-    cross(1)
-    table_copy.wait()
-
-    @pl.when(z0 < 2)
-    def _():
-        transform(0, 2)
-        send_share(z0 // 2)
-
-    @pl.when(outer)
+    part(0, 1 - c0)
+
+    @pl.when(z0 < 3)
+    def _():
+        arrive(3)
+
+    @pl.when(z0 == 0)
     def _():
         arrive(2)
 
+    @pl.when(z0 < 3)
+    def _():
+        cross(1, c0)
+
     core_copy(2, 1 - c0).wait_recv()
-    cross(2)
-    arrive(3)
     core_copy(3, 1 - c0).wait_recv()
-    cross(3)
-    transform(2, 4)
-    send_share(1 - z0 // 2)
-
-    @pl.when(z0 >= 2)
-    def _():
-        transform(0, 2)
-        send_share(z0 // 2)
+    transform(1, c0)
+    send_share(1, c0)
+    part(1, 1 - c0)
 
     for step in (2, 1, 3):
         hour_copy(step, x0).start()
@@ -384,15 +403,23 @@
     def _():
         pl.semaphore_wait(ready, 4)
         for step in (2, 1, 3, 0):
-            ref_copy(step, 1, day).start()
+            for core in range(2):
+                ref_copy(step, 1, core, day).start()
 
     for step in (1, 3, 2):
         hour_copy(step, (x0 - step + 4) % 4).wait_recv()
     for x in range(4):
-        for h in range(2):
-            got = hour_recv[x, h].astype(jnp.float32)
-            hour_wide[x * 128 + h * 64 : x * 128 + h * 64 + 64, :] = got[0:64]
-            hour_rest[x * 32 + h * 16 : x * 32 + h * 16 + 16, :] = got[64:80]
+        for core in range(2):
+            for h in range(2):
+                got = hour_recv[x, core, h].astype(jnp.float32)
+                for bit in range(2):
+                    for half in range(2):
+                        tile = bit * 2 + half
+                        t = (h * 2 + bit) * 2 + core
+                        first = x * 128 + t * 16 + half * 8
+                        hour_wide[first : first + 8, :] = got[tile * 8 : tile * 8 + 8]
+                        first = x * 32 + t * 4 + half * 2
+                        hour_rest[first : first + 2, :] = got[32 + tile * 2 : 34 + tile * 2]
 
     def hour_tile(x, half, p):
         if p < 8:
@@ -411,16 +438,24 @@
                     0, p, 0, pair * 16 : pair * 16 + 16, half * LANES : (half + 1) * LANES
                 ] = jnp.concatenate(tiles, axis=0).astype(jnp.bfloat16)
 
-    for d in range(8):
-
-        @pl.when(jnp.logical_not(jnp.logical_and(mine, day == d)))
-        def _():
-            ref_copy(1, 0, d).wait_recv()
-
-    summed = ref_recv[0].astype(jnp.float32)
-    for d in range(1, 8):
-        summed = summed + ref_recv[d].astype(jnp.float32)
-    ref_wide[...] = summed
+    for core in range(2):
+        for d in range(8):
+
+            @pl.when(jnp.logical_not(jnp.logical_and(mine, day == d)))
+            def _():
+                ref_copy(1, 0, core, d).wait_recv()
+
+    for core in range(2):
+        summed = ref_recv[core * 8].astype(jnp.float32)
+        for d in range(1, 8):
+            summed = summed + ref_recv[core * 8 + d].astype(jnp.float32)
+        for bit in range(2):
+            for half in range(2):
+                tile = bit * 2 + half
+                first = (bit * 2 + core) * 16 + half * 8
+                ref_wide[first : first + 8, :] = summed[tile * 8 : tile * 8 + 8]
+                first = 64 + (bit * 2 + core) * 4 + half * 2
+                ref_wide[first : first + 2, :] = summed[32 + tile * 2 : 34 + tile * 2]
 
     def share(half, p):
         if p < 8:
@@ -447,14 +482,16 @@
         x_copy(step, x0).wait_send()
         hour_copy(step, x0).wait_send()
         for h in range(2):
-            ref_copy(step, h, day).wait_send()
-    for i in range(4):
-        core_copy(i, c0).wait_send()
+            for core in range(2):
+                ref_copy(step, h, core, day).wait_send()
+    for z in range(4):
+        core_copy(z, c0).wait_send()
     for h in range(2):
 
         @pl.when(jnp.logical_not(jnp.logical_and(mine, h0 == h)))
         def _():
-            ref_copy(0, h, day).wait_send()
+            for core in range(2):
+                ref_copy(0, h, core, day).wait_send()
 
 
 def write_out(hourly_ref, stack_ref, hourly_hbm, stack_hbm, sems):
@@ -502,9 +539,9 @@
             vmem((8 * BLOCK, LANES), f32),
             vmem((32, LANES), f32),
             vmem((8, LANES), f32),
-            vmem((4, 2, BLOCK, LANES), bf16),
-            vmem((4, 2, BLOCK, LANES), bf16),
-            vmem((8, BLOCK, LANES), bf16),
+            vmem((4, 2, 2, 48, LANES), bf16),
+            vmem((4, 2, 2, 48, LANES), bf16),
+            vmem((16, 48, LANES), bf16),
             vmem((4 * 128, LANES), f32),
             vmem((4 * 32, LANES), f32),
             vmem((BLOCK, LANES), f32),
@@ -519,8 +556,8 @@
             dma((4,)),
             dma((4,)),
             dma((4,)),
-            dma((4, 2)),
-            dma((8,)),
+            dma((4, 2, 2)),
+            dma((16,)),
             pltpu.SemaphoreType.REGULAR,
         ],
         compiler_params=pltpu.CompilerParams(

time: 27 us -> 26.6 us (0.985)
  Pallas kernels: 26.2 us -> 25.8 us
    pallas_call x1, Pallas kernels: 25.5 us -> 25.1 us  [on_device(): pl.pallas_call(kernel, out_shape=shapes, in_specs=[pl.BlockSpec(memory_sp...]
where the time goes in v5:
time: 26.6 us; the launch traced here: 26.5 us
  Pallas kernels  25.8 us (97%)
  between operations  0.64 us (2%)
    pallas_call x1, Pallas kernels, on_device(): pl.pallas_call(kernel, out_shape=shapes, in_specs=[pl.BlockSpec(memory_sp...  25.1 us
    pallas_call x1, Pallas kernels, on_device(): pl.pallas_call(write_out, out_shape=shapes, in_specs=[pl.BlockSpec(memory...  0.69 us

profile of v5, /device:TPU:96, one launch (start us, length us, event | category | flops | bytes accessed | tf_op | source)
XLA Modules:
  0.0 26.5 jit_solution(2533623827593191970)
XLA Ops:
  0.6 25.1 %shard_map.59 = (bf16[1,9,1,32,256]{4,3,2,1,0:T(8,128)(2,1)S(1)}, f32[9,1,4,256]{3,2,1,0:T(4,128)S(1)}) custom-call(bf16[1,2,3,4,1536]{4,3,2,1,0:T(4,128)(2,1)} %bitcast.1, s32[1,4]{1,0:T(1,128)} %flags_hbm.1, s32[1,32]{1,0:T(1,128)} %mask_hbm.1, bf16[3072,256]{1,0:T(8,128)(2,1)} %constant.2.clone.table_hbm), custom_call_target="tpu_custom_call" | custom-call | flops 500000000 | bytes 2000000 | tf_op jit(solution)/shard_map/pallas_call | solution.py:518
  25.8 0.7 %shard_map.60 = (bf16[1,9,1,32,256]{4,3,2,1,0:T(8,128)(2,1)}, f32[9,1,4,256]{3,2,1,0:T(4,128)}) custom-call(bf16[1,9,1,32,256]{4,3,2,1,0:T(8,128)(2,1)S(1)} %get-tuple-element.4.hourly_ref, f32[9,1,4,256]{3,2,1,0:T(4,128)S(1)} %get-tuple-element.5.stack_ref), custom_call_target="tpu_custom_call" | custom-call | tf_op jit(solution)/shard_map/pallas_call | solution.py:570

commit v6 on v5

--- a/solution.py
+++ b/solution.py
@@ -360,10 +360,6 @@
 
     table_copy.wait()
 
-    @pl.when(z0 == 3)
-    def _():
-        cross(1, c0)
-
     @pl.when(z0 >= 2)
     def _():
         arrive(0)
@@ -385,9 +381,7 @@
     def _():
         arrive(2)
 
-    @pl.when(z0 < 3)
-    def _():
-        cross(1, c0)
+    cross(1, c0)
 
     core_copy(2, 1 - c0).wait_recv()
     core_copy(3, 1 - c0).wait_recv()

time: 26.6 us -> 26.3 us (0.989)
  the two profiles are of different devices: /device:TPU:96 before, /device:TPU:1 now
where the time goes in v6:
time: 26.3 us; the launch traced here: 25.9 us
  Pallas kernels  25.3 us (96%)
  between operations  0.64 us (2%)
    pallas_call x1, Pallas kernels, on_device(): pl.pallas_call(kernel, out_shape=shapes, in_specs=[pl.BlockSpec(memory_sp...  24.6 us
    pallas_call x1, Pallas kernels, on_device(): pl.pallas_call(write_out, out_shape=shapes, in_specs=[pl.BlockSpec(memory...  0.69 us

profile of v6, /device:TPU:1, one launch (start us, length us, event | category | flops | bytes accessed | tf_op | source)
XLA Modules:
  0.0 25.9 jit_solution(10452989009734526718)
XLA Ops:
  0.6 24.6 %shard_map.59 = (bf16[1,9,1,32,256]{4,3,2,1,0:T(8,128)(2,1)S(1)}, f32[9,1,4,256]{3,2,1,0:T(4,128)S(1)}) custom-call(bf16[1,2,3,4,1536]{4,3,2,1,0:T(4,128)(2,1)} %bitcast.1, s32[1,4]{1,0:T(1,128)} %flags_hbm.1, s32[1,32]{1,0:T(1,128)} %mask_hbm.1, bf16[3072,256]{1,0:T(8,128)(2,1)} %constant.2.clone.table_hbm), custom_call_target="tpu_custom_call" | custom-call | flops 500000000 | bytes 2000000 | tf_op jit(solution)/shard_map/pallas_call | solution.py:512
  25.3 0.7 %shard_map.60 = (bf16[1,9,1,32,256]{4,3,2,1,0:T(8,128)(2,1)}, f32[9,1,4,256]{3,2,1,0:T(4,128)}) custom-call(bf16[1,9,1,32,256]{4,3,2,1,0:T(8,128)(2,1)S(1)} %get-tuple-element.4.hourly_ref, f32[9,1,4,256]{3,2,1,0:T(4,128)S(1)} %get-tuple-element.5.stack_ref), custom_call_target="tpu_custom_call" | custom-call | tf_op jit(solution)/shard_map/pallas_call | solution.py:564
